TPU v7x, 32 devices: a whole 2x2x4 slice. The times are simulated.
32 devices in a mesh: axial: 4 (over x, core), azim: 8 (over z, y).
Axes of the slice: x: 2, y: 2, z: 4, core: 2. Of those that a mesh axis runs over, the one named last changes fastest.
Arguments:
- cycle_state: float32 [5, 32, 1024, 256], P(None, 'axial', 'azim'), as said below
- core_state: float32 [5, 32, 192, 192], P(None, 'axial', 'azim'), as said below
- core_taps: int32 [768, 4], replicated, may hold values from 0 to 1023, as said below
- core_weights: float32 [768, 4], replicated, may hold values from 0.1 to 1
- cycle_taps: int32 [1024, 4], replicated, may hold values from 0 to 36863, as said below
- cycle_weights: float32 [1024, 4], replicated, may hold values from 0.1 to 1
Outputs:
- cycle_new: float32 [5, 32, 1024, 256], P(None, 'axial', 'azim')
- core_new: float32 [5, 32, 192, 192], P(None, 'axial', 'azim')
Inputs may be any that keep to these rules, and one draw needn't show every extreme that they name: `core_taps`: cycle positions, each within 8 positions (cyclically) of position g * 1024 // 768. `cycle_taps`: flat indices of core cells within three cells of the core's edge. `cycle_state`: density (component 0) lies in 0.5 to 1.5. `core_state`: density (component 0) lies in 0.5 to 1.5.
All inputs are finite; a program needn't handle non-finite values.
Results may differ from a plain program's by a relative error of at most 0.0003.
Values sent between devices are 32-bit elements; how exact they have to be, the bound alone decides.
No kernel may reach another device: no remote copies, remote signals or barrier semaphores. Data moves between devices by JAX's collectives and lax.ppermute only.
A program may use at most 128 MiB of HBM per device.

v0:
```python
import math

import jax
import jax.numpy as jnp
from jax import lax
from jax.sharding import PartitionSpec as P

time_step = 0.001
axial_step = 0.004
radial_step = 1.0 / 256.0
core_step = 2.0 / 192.0
inner_radius = 1.0
viscosity = 0.002
gamma_minus = 0.4


def padded_2(block, sides, width):
    for axis, dim in sides:
        count = lax.axis_size(axis)
        forward = [(i, i + 1) for i in range(count - 1)]
        forward.append((count - 1, 0))
        backward = [(target, source) for source, target in forward]
        low = lax.ppermute(
            lax.slice_in_dim(block, block.shape[dim] - width, None, axis=dim), axis, forward
        )
        high = lax.ppermute(lax.slice_in_dim(block, 0, width, axis=dim), axis, backward)
        block = jnp.concatenate([low, block, high], axis=dim)
    return block


def pressure_of(state):
    kinetic = 0.5 * (state[1] * state[1] + state[2] * state[2] + state[3] * state[3]) / state[0]
    return gamma_minus * (state[4] - kinetic)


def fluxes(state, component):
    pressure = pressure_of(state)
    velocity = state[component] / state[0]
    parts = [
        state[component],
        state[1] * velocity,
        state[2] * velocity,
        state[3] * velocity,
        (state[4] + pressure) * velocity,
    ]
    parts[component] = parts[component] + pressure
    return jnp.stack(parts, axis=0)


def angle_of(positions, total):
    return (positions.astype(jnp.float32) + 0.5) * (2.0 * math.pi / total)


def to_cartesian(trace, angles):
    cosine = jnp.cos(angles)
    sine = jnp.sin(angles)
    y_part = trace[3] * cosine - trace[2] * sine
    z_part = trace[3] * sine + trace[2] * cosine
    return jnp.stack([trace[0], trace[1], y_part, z_part, trace[4]], axis=0)


def to_polar(trace, angles):
    cosine = jnp.cos(angles)
    sine = jnp.sin(angles)
    azimuthal = trace[3] * cosine - trace[2] * sine
    radial = trace[2] * cosine + trace[3] * sine
    return jnp.stack([trace[0], trace[1], azimuthal, radial, trace[4]], axis=0)


def normalized(weights):
    return weights / jnp.sum(weights, axis=1, keepdims=True)


def tap_matrix(taps, weights, offset, count):
    sources = jnp.arange(count, dtype=jnp.int32)[:, None]
    local_idx = taps - offset
    matrix = jnp.zeros((count, taps.shape[0]), jnp.float32)
    for which in range(taps.shape[1]):
        hits = sources == local_idx[:, which][None, :]
        matrix = matrix + jnp.where(hits, weights[:, which][None, :], 0.0)
    return matrix


def apply_taps(values, matrix):
    lead = values.shape[:2]
    flat_values = values.reshape(lead[0] * lead[1], values.shape[2])
    result = jnp.dot(
        flat_values, matrix, preferred_element_type=jnp.float32, precision=lax.Precision.HIGHEST
    )
    return result.reshape(lead[0], lead[1], matrix.shape[1])


def radius_full(count):
    return inner_radius + (jnp.arange(count + 2).astype(jnp.float32) - 0.5) * radial_step


def cycle_rhs(padded, inner_ghost, angle_step):
    center = padded[:, 1:-1, 1:-1]
    reflect = jnp.array([1.0, 1.0, 1.0, -1.0, 1.0], jnp.float32)[:, None, None]
    outer_ghost = center[:, :, :, -1] * reflect
    radial_pad = jnp.concatenate([inner_ghost[..., None], center, outer_ghost[..., None]], axis=3)
    radius = radius_full(center.shape[3])
    mid_radius = radius[1:-1]
    arc = angle_step * mid_radius
    axial_flux = fluxes(padded[:, :, 1:-1], 1)
    azim_flux = fluxes(padded[:, 1:-1], 2)
    radial_flux = fluxes(radial_pad, 3)
    divergence = (axial_flux[:, 2:] - axial_flux[:, :-2]) / (2.0 * axial_step)
    divergence = divergence + (azim_flux[:, :, 2:] - azim_flux[:, :, :-2]) / (2.0 * arc)
    divergence = divergence + (
        radius[2:] * radial_flux[..., 2:] - radius[:-2] * radial_flux[..., :-2]
    ) / (2.0 * radial_step * mid_radius)
    laplace = (padded[:, 2:, 1:-1] - 2.0 * center + padded[:, :-2, 1:-1]) / (
        axial_step * axial_step
    )
    laplace = laplace + (padded[:, 1:-1, 2:] - 2.0 * center + padded[:, 1:-1, :-2]) / (arc * arc)
    laplace = laplace + (radial_pad[..., 2:] - 2.0 * center + radial_pad[..., :-2]) / (
        radial_step * radial_step
    )
    pressure = pressure_of(center)
    swirl = -center[2] * center[3] / (center[0] * mid_radius)
    outward = (center[2] * center[2] / center[0] + pressure) / mid_radius
    zero_part = jnp.zeros_like(swirl)
    source = jnp.stack([zero_part, zero_part, swirl, outward, zero_part], axis=0)
    return -divergence + source + viscosity * laplace


def core_rhs(axial_pad, row_pad, left_col, right_col):
    center = axial_pad[:, 1:-1]
    col_pad = jnp.concatenate([left_col[..., None], center, right_col[..., None]], axis=3)
    axial_flux = fluxes(axial_pad, 1)
    row_flux = fluxes(row_pad, 2)
    col_flux = fluxes(col_pad, 3)
    divergence = (axial_flux[:, 2:] - axial_flux[:, :-2]) / (2.0 * axial_step)
    divergence = divergence + (row_flux[:, :, 2:] - row_flux[:, :, :-2]) / (2.0 * core_step)
    divergence = divergence + (col_flux[..., 2:] - col_flux[..., :-2]) / (2.0 * core_step)
    laplace = (axial_pad[:, 2:] - 2.0 * center + axial_pad[:, :-2]) / (axial_step * axial_step)
    laplace = laplace + (row_pad[:, :, 2:] - 2.0 * center + row_pad[:, :, :-2]) / (
        core_step * core_step
    )
    laplace = laplace + (col_pad[..., 2:] - 2.0 * center + col_pad[..., :-2]) / (
        core_step * core_step
    )
    return -divergence + viscosity * laplace


def body(cycle_state, core_state, core_taps, core_weights, cycle_taps, cycle_weights):
    channels, planes, sector, radial_cells = cycle_state.shape
    core_rows = core_state.shape[2]
    core_cells = core_state.shape[3]
    n_azim = lax.axis_size("azim")
    own_index = lax.axis_index("azim")
    positions_all = sector * n_azim
    angle_step = 2.0 * math.pi / positions_all
    angles = angle_of(own_index * sector + jnp.arange(sector, dtype=jnp.int32), positions_all)
    cart_trace = to_cartesian(cycle_state[:, :, :, 0], angles)
    core_norm = normalized(core_weights)
    all_traces = lax.all_gather(cart_trace, "azim", axis=2, tiled=True)
    ghost_matrix = tap_matrix(core_taps, core_norm, 0, positions_all)
    ghosts = apply_taps(all_traces, ghost_matrix)
    flat_core = core_state.reshape(channels, planes, core_rows * core_cells)
    cycle_matrix = tap_matrix(
        cycle_taps,
        normalized(cycle_weights),
        own_index * core_rows * core_cells,
        core_rows * core_cells,
    )
    cycle_share = apply_taps(flat_core, cycle_matrix)
    inner_cart = lax.psum_scatter(cycle_share, "azim", scatter_dimension=2, tiled=True)
    inner_ghost = to_polar(inner_cart, angles)
    core_pad = padded_2(core_state, (("axial", 1), ("azim", 2)), 1)
    lower = jnp.where(
        own_index == 0, ghosts[:, :, 2 * core_cells : 3 * core_cells], core_pad[:, 1:-1, 0, :]
    )
    upper = jnp.where(
        own_index == n_azim - 1,
        ghosts[:, :, 3 * core_cells : 4 * core_cells],
        core_pad[:, 1:-1, -1, :],
    )
    row_pad = jnp.concatenate([lower[:, :, None], core_state, upper[:, :, None]], axis=2)
    left_col = lax.dynamic_slice_in_dim(ghosts, own_index * core_rows, core_rows, 2)
    right_col = lax.dynamic_slice_in_dim(ghosts, core_cells + own_index * core_rows, core_rows, 2)
    axial_pad = core_pad[:, :, 1:-1, :]
    core_new = core_state + time_step * core_rhs(axial_pad, row_pad, left_col, right_col)
    padded = padded_2(cycle_state, (("axial", 1), ("azim", 2)), 1)
    cycle_new = cycle_state + time_step * cycle_rhs(padded, inner_ghost, angle_step)
    return (cycle_new, core_new)


def solution(mesh):
    placed = (P(None, "axial", "azim", None), P(None, "axial", "azim", None), P(), P(), P(), P())
    return jax.shard_map(
        body,
        mesh=mesh,
        in_specs=placed,
        out_specs=(P(None, "axial", "azim", None), P(None, "axial", "azim", None)),
        check_vma=False,
    )
```

profile of v0, /device:TPU:0, one launch (start us, length us, event | category | flops | bytes accessed | tf_op | source)
XLA Modules:
  0.0 201.2 jit_solution(3539996914909524414)
XLA Ops:
  7.2 1.5 reshape_reshape.3
  11.0 18.4 %fusion.57 = f32[5,8,1024]{2,1,0:T(8,128)} fusion(f32[40,4608]{1,0:T(8,128)S(1)} %reshape_reshape.3, f32[1024]{0:T(1024)S(1)} %bitcast.71, s32[1024]{0:T(1024)S(1)} %bitcast.75, f32[1024]{0:T(1024)S(1)} %bitcast.72, s32[1024]{0:T(1024)S(1)} %bitcast.76, f32[1024]{0:T(1024)S(1)} %bitcast.73, s32[1024]{0:T(1024)S(1)} %bitcast.77, f32[1024]{0:T(1024)S(1)} %bitcast.70, ...), kind=kOutput, calls=%fused_computation.92 | convolution fusion | flops 2316828672 | bytes 933888 | tf_op jit(solution)/shard_map/dot_general | solution.py:87
  29.4 2.5 %fusion.92 = (f32[5,1,128,256]{3,2,1,0:T(8,128)}, f32[5,1,128,256]{3,2,1,0:T(8,128)}) fusion(f32[5,8,128,256]{3,2,1,0:T(8,128)} %param.7), kind=kLoop, calls=%fused_computation.210 | loop fusion | bytes 2621440 | tf_op jit(solution)/shard_map/slice | solution.py:26
  32.4 1.9 collective-permute-start.1
  36.5 2.9 %fusion.91 = (f32[1,8,128,1]{3,2,1,0:T(8,128)S(1)}, f32[1,8,128,1]{3,2,1,0:T(8,128)S(1)}, f32[1,8,128,1]{3,2,1,0:T(8,128)}, f32[1,8,128,1]{3,2,1,0:T(8,128)S(1)}, f32[1,8,128,1]{3,2,1,0:T(8,128)}) fusion(f32[5,8,128,256]{3,2,1,0:T(8,128)} %param.7), kind=kLoop, calls=%fused_computation.209 | loop fusion | bytes 40960 | tf_op jit(solution)/shard_map/slice | solution.py:59
  39.8 1.2 copy.55
  41.0 1.2 copy.56
  42.6 4.0 %slice_multiply_fusion.2 = f32[5,8,128,1]{3,2,1,0:T(8,128)} fusion(f32[5,8,128,256]{3,2,1,0:T(8,128)} %param.7, f32[5]{0:T(128)S(1)} %copy-done.17), kind=kLoop, calls=%fused_computation.68 | loop fusion | flops 5120 | bytes 40980 | tf_op jit(solution)/shard_map/mul | solution.py:100
  47.3 4.5 %multiply_divide_fusion = (f32[1,8,128,256]{3,2,1,0:T(8,128)}, f32[1,8,128,256]{3,2,1,0:T(8,128)}) fusion(f32[5,8,128,256]{3,2,1,0:T(8,128)} %param.7, f32[256]{0:T(256)S(1)} %get-tuple-element.75), kind=kLoop, calls=%fused_computation.107 | loop fusion | flops 4194304 | bytes 7341056 | tf_op jit(solution)/shard_map/div | solution.py:121
  52.8 1.4 pad_maximum_fusion.22
  54.3 5.2 %collective-permute-start.7 = (f32[5,10,1,192]{3,1,0,2:T(8,128)}, f32[5,10,1,192]{3,1,0,2:T(8,128)}, u32[]{:S(2)}, u32[]{:S(2)}) collective-permute-start(f32[5,10,1,192]{3,1,0,2:T(8,128)} %get-tuple-element.51), channel_id=1, source_target_pairs={{1,0},{2,1},{3,2},{4,3},{5,4},{6,5},{7,6},{0,7},{9,8},{10,9},{11,1... | collective-permute-start | bytes 115208 | tf_op jit(solution)/shard_map/ppermute | solution.py:26
  59.5 1.4 pad_maximum_fusion.7
  65.2 21.7 %reduce-scatter.2.cloned.1.call-done = f32[5,8,128]{2,1,0:T(8,128)} async-done(((f32[5,8,1024]{2,1,0:T(8,128)}), f32[5,8,128]{2,1,0:T(8,128)}) %reduce-scatter.2.cloned.1.call-update) | async-done | bytes 20496 | tf_op jit(solution)/shard_map/reduce_scatter | solution.py:169
  88.3 2.3 %copy.30 = f32[5,8,128,1]{3,2,1,0:T(8,128)} copy(f32[5,8,128,1]{2,1,0,3:T(8,128)S(1)} %maximum_bitcast_fusion) | data formatting | bytes 40960 | tf_op jit(solution)/shard_map/broadcast_in_dim | solution.py:101
  90.5 6.0 %pad_maximum_fusion = f32[5,8,128,258]{3,2,1,0:T(8,128)S(1)} fusion(f32[5,8,128,1]{3,2,1,0:T(8,128)} %slice_multiply_fusion.2, f32[5,8,128,256]{3,2,1,0:T(8,128)} %param.7, f32[5,8,128,1]{3,2,1,0:T(8,128)} %copy.30), kind=kLoop, calls=%fused_computation.21 | loop fusion | flops 2641920 | bytes 10567680 | tf_op jit(solution)/shard_map/concatenate | solution.py:101
  97.0 2.7 %copy-done = f32[5,8,128,258]{3,2,1,0:T(8,128)} copy-done((f32[5,8,128,258]{3,2,1,0:T(8,128)}, f32[5,8,128,258]{3,2,1,0:T(8,128)S(1)}, u32[]{:S(2)}) %copy-start) | copy-done | bytes 5283864
  99.7 3.1 %copy-done.4 = f32[5,8,128,258]{3,2,1,0:T(8,128)} copy-done((f32[5,8,128,258]{3,2,1,0:T(8,128)}, f32[5,8,128,258]{3,2,1,0:T(8,128)S(1)}, u32[]{:S(2)}) %copy-start.4) | copy-done | bytes 5283864
  102.8 30.6 %all_gather.3 = f32[5,8,1024]{2,1,0:T(8,128)S(1)} all-gather(f32[5,8,128]{2,1,0:T(8,128)S(1)} %constant_dynamic-update-slice_fusion.4), channel_id=1, replica_groups=mesh['axial'=4,'azim'=8] {'azim'}, dimensions={2}, use_global_device_ids=true | all-gather | bytes 184320 | tf_op jit(solution)/shard_map/all_gather | solution.py:158
  133.4 3.4 %fusion.39 = f32[5,8,768]{2,1,0:T(8,128)S(1)} fusion(f32[5,8,1024]{2,1,0:T(8,128)S(1)} %all_gather.3, f32[768]{0:T(1024)S(1)} %get-tuple-element.11, s32[768]{0:T(1024)S(1)} %get-tuple-element.8, f32[768]{0:T(1024)S(1)} %get-tuple-element.12, s32[768]{0:T(1024)S(1)} %get-tuple-element.9, f32[768]{0:T(1024)S(1)} %get-tuple-element.13, ...), kind=kOutput, calls=%fused_computation.55 | convolution fusion | flops 386138112 | bytes 311296 | tf_op jit(solution)/shard_map/dot_general | solution.py:87
  137.8 1.0 copy.43
  139.7 1.0 fusion.81
  141.2 3.7 %fusion.66 = f32[5,8,24,192]{3,1,0,2:T(8,128)S(1)} fusion(f32[5,8,24,192]{3,1,0,2:T(8,128)S(1)} %copy.53, f32[5,8,24,1]{3,1,0,2:T(8,128)S(1)} %copy.41, f32[5,8,24,1]{3,1,0,2:T(8,128)S(1)} %copy.43, f32[5,8,1,192]{3,1,0,2:T(8,128)S(1)} %get-tuple-element.56, f32[5,8,1,192]{3,1,0,2:T(8,128)S(1)} %get-tuple-element.55, ...), kind=kLoop, calls=%fused_computation.115 | loop fusion | flops 5713920 | bytes 6151680 | tf_op jit(solution)/shard_map/add | solution.py:184
  144.8 1.3 copy.54
  146.1 1.4 multiply_dynamic-update-slice_fusion.1
  147.5 1.9 add_dynamic-update-slice_fusion
  149.4 1.5 multiply_dynamic-update-slice_fusion
  150.8 1.1 constant_dynamic-update-slice_fusion.2
  153.0 1.1 constant_dynamic-update-slice_fusion
  154.4 4.7 %collective-permute-start.3 = (f32[5,10,1,256]{3,2,1,0:T(1,128)S(1)}, f32[5,10,1,256]{3,2,1,0:T(1,128)S(1)}, u32[]{:S(2)}, u32[]{:S(2)}) collective-permute-start(f32[5,10,1,256]{3,2,1,0:T(1,128)S(1)} %get-tuple-element.40), channel_id=1, source_target_pairs={{1,0},{2,1},{3,2},{4,3},{5,4},{6,5},{7,6},{0,7},{9,8},{10,9},{11,1... | collective-permute-start | bytes 153608 | tf_op jit(solution)/shard_map/ppermute | solution.py:26
  161.2 1.9 copy-done.3
  165.0 2.8 %copy-done.1 = f32[5,8,130,256]{3,2,1,0:T(8,128)} copy-done((f32[5,8,130,256]{3,2,1,0:T(8,128)}, f32[5,8,130,256]{3,2,1,0:T(8,128)S(1)}, u32[]{:S(2)}) %copy-start.1) | copy-done | bytes 5324824
  168.8 25.5 %fusion.23 = f32[5,8,128,256]{3,2,1,0:T(8,128)} fusion(f32[5,8,128,256]{3,2,1,0:T(8,128)} %param.7, f32[5,8,128,1]{3,2,1,0:T(8,128)S(1)} %copy-done.2, f32[5,8,128,1]{3,2,1,0:T(8,128)} %slice_multiply_fusion.2, f32[5,10,128,256]{3,2,1,0:T(8,128)S(1)} %constant_dynamic-update-slice_fusion, f32[5,10,1,256]{3,2,1,0:T(1,128)S(1)} %collective-permute-done.2, ...), kind=kLoop, calls=%fused_computation.29 | loop fusion | flops 48496640 | bytes 52053032 | tf_op jit(solution)/shard_map/add | solution.py:186
  (119 shorter events, 21.8 us)
Async XLA Ops:
  7.2 79.7 %reduce-scatter.2.cloned.1.call-start = ((), (), s32[]{:S(2)}) async-start(), calls=%async_computation.1 | async-start | bytes 184320 | tf_op jit(solution)/shard_map/reduce_scatter | solution.py:169
  29.4 4.9 %copy-start.5 = (f32[5,8,24,192]{3,2,1,0:T(8,128)S(1)}, f32[5,8,24,192]{3,2,1,0:T(8,128)}, u32[]{:S(2)}) copy-start(f32[5,8,24,192]{3,2,1,0:T(8,128)} %param.8) | copy-start | bytes 2211844
  31.9 118.9 %collective-permute-start = (f32[5,1,128,256]{3,2,1,0:T(8,128)}, f32[5,1,128,256]{3,2,1,0:T(8,128)}, u32[]{:S(2)}, u32[]{:S(2)}) collective-permute-start(f32[5,1,128,256]{3,2,1,0:T(8,128)} %get-tuple-element.50), channel_id=1, source_target_pairs={{0,8},{8,16},{16,24},{24,0},{1,9},{9,17},{17,25},{25,1},{2,10},{10... | collective-permute-start | bytes 1966088 | tf_op jit(solution)/shard_map/ppermute | solution.py:23
  32.4 120.6 %collective-permute-start.1 = (f32[5,1,128,256]{3,2,1,0:T(8,128)}, f32[5,1,128,256]{3,2,1,0:T(8,128)}, u32[]{:S(2)}, u32[]{:S(2)}) collective-permute-start(f32[5,1,128,256]{3,2,1,0:T(8,128)} %get-tuple-element.49), channel_id=1, source_target_pairs={{8,0},{16,8},{24,16},{0,24},{9,1},{17,9},{25,17},{1,25},{10,2},{18... | collective-permute-start | bytes 1966088 | tf_op jit(solution)/shard_map/ppermute | solution.py:26
  35.1 17.7 %collective-permute-start.5 = (f32[5,1,24,192]{3,1,0,2:T(1,128)}, f32[5,1,24,192]{3,1,0,2:T(1,128)}, u32[]{:S(2)}, u32[]{:S(2)}) collective-permute-start(f32[5,1,24,192]{3,1,0,2:T(1,128)} %copy.33), channel_id=1, source_target_pairs={{8,0},{16,8},{24,16},{0,24},{9,1},{17,9},{25,17},{1,25},{10,2},{18... | collective-permute-start | bytes 276488 | tf_op jit(solution)/shard_map/ppermute | solution.py:26
  36.5 16.3 %collective-permute-start.4 = (f32[5,1,24,192]{3,1,0,2:T(1,128)}, f32[5,1,24,192]{3,1,0,2:T(1,128)}, u32[]{:S(2)}, u32[]{:S(2)}) collective-permute-start(f32[5,1,24,192]{3,1,0,2:T(1,128)} %copy.32), channel_id=1, source_target_pairs={{0,8},{8,16},{16,24},{24,0},{1,9},{9,17},{17,25},{25,1},{2,10},{10... | collective-permute-start | bytes 276488 | tf_op jit(solution)/shard_map/ppermute | solution.py:23
  39.4 3.2 %copy-start.17 = (f32[5]{0:T(128)S(1)}, f32[5]{0:T(128)}, u32[]{:S(2)}) copy-start(f32[5]{0:T(128)} %constant.21.clone) | copy-start | bytes 64
  47.3 5.3 %copy-start.10 = (f32[768,4]{0,1:T(4,128)S(1)}, f32[768,4]{0,1:T(4,128)}, u32[]{:S(2)}) copy-start(f32[768,4]{0,1:T(4,128)} %param.10) | copy-start | bytes 36868
  47.3 5.5 %copy-start.13 = (s32[768,4]{0,1:T(4,128)S(1)}, s32[768,4]{0,1:T(4,128)}, u32[]{:S(2)}) copy-start(s32[768,4]{0,1:T(4,128)} %param.9) | copy-start | bytes 36868
  54.3 85.2 %collective-permute-start.7 = (f32[5,10,1,192]{3,1,0,2:T(8,128)}, f32[5,10,1,192]{3,1,0,2:T(8,128)}, u32[]{:S(2)}, u32[]{:S(2)}) collective-permute-start(f32[5,10,1,192]{3,1,0,2:T(8,128)} %get-tuple-element.51), channel_id=1, source_target_pairs={{1,0},{2,1},{3,2},{4,3},{5,4},{6,5},{7,6},{0,7},{9,8},{10,9},{11,1... | collective-permute-start | bytes 115208 | tf_op jit(solution)/shard_map/ppermute | solution.py:26
  59.5 80.0 %collective-permute-start.6 = (f32[5,10,1,192]{3,1,0,2:T(8,128)}, f32[5,10,1,192]{3,1,0,2:T(8,128)}, u32[]{:S(2)}, u32[]{:S(2)}) collective-permute-start(f32[5,10,1,192]{3,1,0,2:T(8,128)} %get-tuple-element.52), channel_id=1, source_target_pairs={{0,1},{1,2},{2,3},{3,4},{4,5},{5,6},{6,7},{7,0},{8,9},{9,10},{10,1... | collective-permute-start | bytes 115208 | tf_op jit(solution)/shard_map/ppermute | solution.py:23
  88.3 8.3 %copy-start.11 = (f32[5,8,128]{2,1,0:T(8,128)}, f32[5,8,128]{2,1,0:T(8,128)S(1)}, u32[]{:S(2)}) copy-start(f32[5,8,128]{2,1,0:T(8,128)S(1)} %get-tuple-element.76) | copy-start | bytes 61444
  96.6 3.1 %copy-start = (f32[5,8,128,258]{3,2,1,0:T(8,128)}, f32[5,8,128,258]{3,2,1,0:T(8,128)S(1)}, u32[]{:S(2)}) copy-start(f32[5,8,128,258]{3,2,1,0:T(8,128)S(1)} %pad_maximum_fusion) | copy-start | bytes 15851524
  96.7 6.1 %copy-start.12 = (f32[5,8,128]{2,1,0:T(8,128)S(1)}, f32[5,8,128]{2,1,0:T(8,128)}, u32[]{:S(2)}) copy-start(f32[5,8,128]{2,1,0:T(8,128)} %copy-done.11) | copy-start | bytes 61444
  99.7 3.1 %copy-start.4 = (f32[5,8,128,258]{3,2,1,0:T(8,128)}, f32[5,8,128,258]{3,2,1,0:T(8,128)S(1)}, u32[]{:S(2)}) copy-start(f32[5,8,128,258]{3,2,1,0:T(8,128)S(1)} %get-tuple-element.38) | copy-start | bytes 15851524
  136.8 0.7 copy-start.8
  138.8 0.9 copy-start.9
  140.9 5.2 %slice-start.2 = ((s8[7864320]{0:T(1024)(128)(4,1)}), s8[4194304]{0:T(1024)(128)(4,1)S(1)}, s32[]{:S(2)}) async-start(s8[7864320]{0:T(1024)(128)(4,1)} %bitcast.68), calls=%async_computation.4 | async-start | bytes 8388608
  141.1 5.0 %slice-start.3 = ((s8[7864320]{0:T(1024)(128)(4,1)}), s8[3670016]{0:T(1024)(128)(4,1)S(1)}, s32[]{:S(2)}) async-start(s8[7864320]{0:T(1024)(128)(4,1)} %bitcast.68), calls=%async_computation.5 | async-start | bytes 7340032
  146.1 5.9 %slice-start = ((s8[5242880]{0:T(1024)(128)(4,1)}), s8[4194304]{0:T(1024)(128)(4,1)S(1)}, s32[]{:S(2)}) async-start(s8[5242880]{0:T(1024)(128)(4,1)} %bitcast.66), calls=%async_computation.2 | async-start | bytes 8388608
  147.5 4.5 %slice-start.1 = ((s8[5242880]{0:T(1024)(128)(4,1)}), s8[1048576]{0:T(1024)(128)(4,1)S(1)}, s32[]{:S(2)}) async-start(s8[5242880]{0:T(1024)(128)(4,1)} %bitcast.66), calls=%async_computation.3 | async-start | bytes 2097152
  154.3 6.9 %collective-permute-start.2 = (f32[5,10,1,256]{3,2,1,0:T(1,128)S(1)}, f32[5,10,1,256]{3,2,1,0:T(1,128)S(1)}, u32[]{:S(2)}, u32[]{:S(2)}) collective-permute-start(f32[5,10,1,256]{3,2,1,0:T(1,128)S(1)} %get-tuple-element.41), channel_id=1, source_target_pairs={{0,1},{1,2},{2,3},{3,4},{4,5},{5,6},{6,7},{7,0},{8,9},{9,10},{10,1... | collective-permute-start | bytes 153608 | tf_op jit(solution)/shard_map/ppermute | solution.py:23
  154.4 8.7 %collective-permute-start.3 = (f32[5,10,1,256]{3,2,1,0:T(1,128)S(1)}, f32[5,10,1,256]{3,2,1,0:T(1,128)S(1)}, u32[]{:S(2)}, u32[]{:S(2)}) collective-permute-start(f32[5,10,1,256]{3,2,1,0:T(1,128)S(1)} %get-tuple-element.40), channel_id=1, source_target_pairs={{1,0},{2,1},{3,2},{4,3},{5,4},{6,5},{7,6},{0,7},{9,8},{10,9},{11,1... | collective-permute-start | bytes 153608 | tf_op jit(solution)/shard_map/ppermute | solution.py:26
  160.3 2.8 %copy-start.3 = (f32[5,10,128,256]{3,2,1,0:T(8,128)}, f32[5,10,128,256]{3,2,1,0:T(8,128)S(1)}, u32[]{:S(2)}) copy-start(f32[5,10,128,256]{3,2,1,0:T(8,128)S(1)} %multiply_dynamic-update-slice_fusion.3) | copy-start | bytes 19660804
  164.5 3.4 %copy-start.2 = (f32[5,8,128,1]{3,2,1,0:T(8,128)S(1)}, f32[5,8,128,1]{3,2,1,0:T(8,128)}, u32[]{:S(2)}) copy-start(f32[5,8,128,1]{3,2,1,0:T(8,128)} %copy.30) | copy-start | bytes 61444
  164.5 3.4 %copy-start.6 = (f32[1,8,128,256]{3,2,1,0:T(8,128)S(1)}, f32[1,8,128,256]{3,2,1,0:T(8,128)}, u32[]{:S(2)}) copy-start(f32[1,8,128,256]{3,2,1,0:T(8,128)} %get-tuple-element.42) | copy-start | bytes 3145732
  164.5 4.3 %copy-start.7 = (f32[1,8,128,256]{3,2,1,0:T(8,128)S(1)}, f32[1,8,128,256]{3,2,1,0:T(8,128)}, u32[]{:S(2)}) copy-start(f32[1,8,128,256]{3,2,1,0:T(8,128)} %get-tuple-element.43) | copy-start | bytes 3145732
  164.5 4.3 %copy-start.14 = (f32[256]{0:T(256)S(1)}, f32[256]{0:T(256)}, u32[]{:S(2)}) copy-start(f32[256]{0:T(256)} %get-tuple-element.73) | copy-start | bytes 3076
  164.5 4.3 %copy-start.15 = (f32[256]{0:T(256)S(1)}, f32[256]{0:T(256)}, u32[]{:S(2)}) copy-start(f32[256]{0:T(256)} %get-tuple-element.74) | copy-start | bytes 3076
  164.5 4.3 %copy-start.16 = (f32[5]{0:T(128)S(1)}, f32[5]{0:T(128)}, u32[]{:S(2)}) copy-start(f32[5]{0:T(128)} %pad.33.clone) | copy-start | bytes 64
  165.0 2.8 %copy-start.1 = (f32[5,8,130,256]{3,2,1,0:T(8,128)}, f32[5,8,130,256]{3,2,1,0:T(8,128)S(1)}, u32[]{:S(2)}) copy-start(f32[5,8,130,256]{3,2,1,0:T(8,128)S(1)} %multiply_dynamic-update-slice_fusion.6) | copy-start | bytes 15974404
Sparse Core Ops, SparseCore 0:
  29.5 57.3 reduce-scatter.1
where the time goes:
time: 202 us; the launch traced here: 201 us
  other arithmetic  63.6 us (31%)
  local copies, waits for them, and re-layouts  35 us (17%)
  blocking collectives  30.6 us (15%)
  waiting for transfers between devices  22.6 us (11%)
  matrix products  21.8 us (11%)
  between operations  14.6 us (7%)
  starting transfers between devices  13.1 us (6%)
    all_gather x1, blocking collectives, body(): all_traces = lax.all_gather(cart_trace, 'azim', axis=2, tiled=True)  30.6 us
    add x1, other arithmetic, body(): cycle_state + time_step * cycle_rhs(padded, inner_ghost, angle_step)  25.5 us
    dot_general x2, matrix products, apply_taps(): jnp.dot(flat_values, matrix, preferred_element_type=jnp.float32, precisio...  21.8 us
    reduce_scatter x1, waiting for transfers between devices, body(): lax.psum_scatter(cycle_share, 'azim', scatter_dimension=2, tiled=True)  21.7 us
    unnamed x60, local copies, waits for them, and re-layouts  19.5 us
    ppermute x4, starting transfers between devices, padded_2(): lax.ppermute(lax.slice_in_dim(block, 0, width, axis=dim), axis, backward)  12.5 us
    unnamed x22, other arithmetic  8.84 us
    concatenate x1, other arithmetic, cycle_rhs(): jnp.concatenate([inner_ghost[..., None], center, outer_ghost[..., None]],...  6.04 us
  transfers between devices with their start and end apart: 9, of which 2 were waited for; matrix products, arithmetic and copies ran while one was open for 29% of the time, Pallas kernels for 0%

commit v1 on v0

v1 whole, which is shorter than its diff:
```python
import functools
import math

import jax
import jax.numpy as jnp
from jax import lax
from jax.experimental import pallas as pl
from jax.experimental.pallas import tpu as pltpu
from jax.sharding import PartitionSpec as P

time_step = 0.001
axial_step = 0.004
radial_step = 1.0 / 256.0
core_step = 2.0 / 192.0
inner_radius = 1.0
viscosity = 0.002
gamma_minus = 0.4

LANES = 128
SUB = 8
PAIR = 64
GRANT = 40 * 1024 * 1024


def in_hbm(x):
    return pltpu.with_memory_space_constraint(x, pltpu.HBM)
f32 = jnp.float32
AX_ALPHA = time_step * viscosity / (axial_step * axial_step)
AX_BETA = time_step / (2.0 * axial_step)
RAD_ALPHA = time_step * viscosity / (radial_step * radial_step)
RAD_BETA = time_step / (2.0 * radial_step)
CORE_ALPHA = time_step * viscosity / (core_step * core_step)
CORE_BETA = time_step / (2.0 * core_step)


def velocities(q):
    inv = 1.0 / q[0]
    u = (q[1] * inv, q[2] * inv, q[3] * inv)
    kinetic = 0.5 * (q[1] * u[0] + q[2] * u[1] + q[3] * u[2])
    pressure = gamma_minus * (q[4] - kinetic)
    return u, pressure, q[4] + pressure


def scaled_flux(q, u, pressure, enthalpy, k, scale):
    su = u[k - 1] * scale
    parts = [q[k] * scale, q[1] * su, q[2] * su, q[3] * su, enthalpy * su]
    parts[k] = parts[k] + pressure * scale
    return parts


def to_sides(q, u, pressure, enthalpy, k, alpha, beta):
    flux = scaled_flux(q, u, pressure, enthalpy, k, beta)
    before, after = [], []
    for c in range(5):
        spread = q[c] * alpha
        before.append(spread - flux[c])
        after.append(spread + flux[c])
    return before, after


def radial_tables(cells):
    lane = lax.broadcasted_iota(jnp.int32, (1, cells), 1).astype(f32)
    radius = inner_radius + (lane + 0.5) * radial_step
    return radius, 1.0 / radius


def azim_coefs(radius_inv, angle_step):
    arc_inv = radius_inv * (1.0 / angle_step)
    return (time_step * viscosity) * arc_inv * arc_inv, (0.5 * time_step) * arc_inv


def edge_rows(q, alpha, beta):
    u, pressure, enthalpy = velocities(q)
    return to_sides(q, u, pressure, enthalpy, 2, alpha, beta)


def all_fluxes(q):
    inv = 1.0 / q[0]
    u1, u2, u3 = q[1] * inv, q[2] * inv, q[3] * inv
    m11, m22, m33 = q[1] * u1, q[2] * u2, q[3] * u3
    m12, m13, m23 = q[1] * u2, q[1] * u3, q[2] * u3
    pressure = gamma_minus * (q[4] - 0.5 * (m11 + m22 + m33))
    enthalpy = q[4] + pressure
    return (
        [q[1], m11 + pressure, m12, m13, enthalpy * u1],
        [q[2], m12, m22 + pressure, m23, enthalpy * u2],
        [q[3], m13, m23, m33 + pressure, enthalpy * u3],
    )


def main_kernel(first, count, angle_step, q_hbm, *rest):
    out_hbm, q_ref, out_ref, next_ref, prev_ref, in_sem, out_sem = rest[-7:]
    planes = q_hbm.shape[1]
    sector, cells = q_hbm.shape[2], q_hbm.shape[3]
    chunks = in_sem.shape[0]
    rows = sector // chunks
    lo = max(first - 1, 0)
    hi = min(first + count + 1, planes)
    strips = cells // LANES

    def in_copy(h, s):
        part = pl.ds(h * rows, rows)
        return pltpu.make_async_copy(
            q_hbm.at[:, pl.ds(lo, hi - lo), part, pl.ds(s * LANES, LANES)],
            q_ref.at[:, :, s, part],
            in_sem.at[h, s],
        )

    def out_copy(h):
        part = pl.ds(h * rows, rows)
        return pltpu.make_async_copy(
            out_ref.at[:, :, part], out_hbm.at[:, pl.ds(first, count), part], out_sem.at[h]
        )

    for h in range(chunks):
        for s in range(strips):
            in_copy(h, s).start()
    unit = 1.0 / AX_BETA
    lane = lax.broadcasted_iota(jnp.int32, (1, LANES), 1)
    first_lane = lane == 0
    last_lane = lane == LANES - 1
    row = lax.broadcasted_iota(jnp.int32, (SUB, 1), 0)
    first_row = row == 0
    last_row = row == SUB - 1
    coefs = []
    for s in range(strips):
        radius = inner_radius + ((lane + s * LANES).astype(f32) + 0.5) * radial_step
        radius_inv = 1.0 / radius
        alpha2, beta2 = azim_coefs(radius_inv, angle_step)
        beta_before = RAD_BETA * radius / (radius - radial_step)
        beta_after = RAD_BETA * radius / (radius + radial_step)
        if s == strips - 1:
            wall = RAD_BETA * (radius + radial_step) / radius
            beta_after = jnp.where(last_lane, wall, beta_after)
        center = 1.0 - 2.0 * AX_ALPHA - 2.0 * RAD_ALPHA - 2.0 * alpha2
        table = (alpha2, beta2, beta_before, beta_after, center, time_step * radius_inv)
        coefs.append([jnp.broadcast_to(t * unit, (SUB, LANES)) for t in table])
    ratio = AX_ALPHA / AX_BETA
    radial_alpha = RAD_ALPHA * unit

    tiles = sector // SUB
    chunk_tiles = tiles // chunks
    zero = jnp.zeros((1, cells), f32)
    for i in range(count):
        for c in range(5):
            prev_ref[i, c, SUB - 1 : SUB, :] = zero
            next_ref[i, c, tiles : tiles + 1, :] = zero

    def edges(h):
        for i in range(count):
            x = first + i - lo
            for s in range(strips):
                alpha2, beta2 = coefs[s][0][:chunk_tiles], coefs[s][1][:chunk_tiles]
                wide = slice(s * LANES, (s + 1) * LANES)
                q = [q_ref[c, x, s, pl.ds(h * rows, chunk_tiles, stride=SUB), :] for c in range(5)]
                before, _ = edge_rows(q, alpha2, beta2)
                q = [
                    q_ref[c, x, s, pl.ds(h * rows + SUB - 1, chunk_tiles, stride=SUB), :]
                    for c in range(5)
                ]
                _, after = edge_rows(q, alpha2, beta2)
                for c in range(5):
                    next_ref[i, c, pl.ds(h * chunk_tiles, chunk_tiles), wide] = before[c]
                    prev_ref[i, c, pl.ds(SUB + h * chunk_tiles, chunk_tiles), wide] = after[c]

    def straight(q):
        return q if abs(ratio - 1.0) < 1e-9 else q * ratio

    def tile(j):
        part = pl.ds(pl.multiple_of(j * SUB, SUB), SUB)

        def load(x):
            return [[q_ref[c, x, s, part, :] for c in range(5)] for s in range(strips)]

        def axial(q, sign):
            flux = all_fluxes(q)[0]
            return [straight(q[c]) + sign * flux[c] for c in range(5)]

        def finish(i, held, before):
            for s in range(strips):
                for c in range(5):
                    value = held[s][c] if before is None else held[s][c] + before[s][c]
                    out_ref[c, i, part, s * LANES : (s + 1) * LANES] = value * AX_BETA

        carry = [axial(q, 1.0) for q in load(0)] if first > 0 else None
        held = None
        for i in range(count):
            q = load(first + i - lo)
            flux = [all_fluxes(q[s]) for s in range(strips)]
            if held is not None:
                finish(
                    i - 1,
                    held,
                    [[straight(q[s][c]) - flux[s][0][c] for c in range(5)] for s in range(strips)],
                )
            total = []
            for s in range(strips):
                alpha2, beta2, _, _, center, source = coefs[s]
                part_sum = [q[s][c] * center for c in range(5)]
                if carry is not None:
                    part_sum = [part_sum[c] + carry[s][c] for c in range(5)]
                wide = slice(s * LANES, (s + 1) * LANES)
                for c in range(5):
                    spread = q[s][c] * alpha2
                    moved = flux[s][1][c] * beta2
                    above = next_ref[i, c, pl.ds(j + 1, 1), :][:, wide]
                    below = prev_ref[i, c, pl.ds(j + SUB - 1, 1), :][:, wide]
                    up = pltpu.roll(spread - moved, SUB - 1, 0)
                    down = pltpu.roll(spread + moved, 1, 0)
                    part_sum[c] = part_sum[c] + (
                        jnp.where(last_row, above, up) + jnp.where(first_row, below, down)
                    )
                part_sum[2] = part_sum[2] - flux[s][1][3] * source
                part_sum[3] = part_sum[3] + flux[s][1][2] * source
                total.append(part_sum)
            carry = [[straight(q[s][c]) + flux[s][0][c] for c in range(5)] for s in range(strips)]
            for c in range(5):
                ups, downs, walls = [], [], None
                for s in range(strips):
                    spread = q[s][c] * radial_alpha
                    outward = spread + flux[s][2][c] * coefs[s][3]
                    ups.append(pltpu.roll(spread - flux[s][2][c] * coefs[s][2], LANES - 1, 1))
                    downs.append(pltpu.roll(outward, 1, 1))
                    walls = -outward if c == 3 else outward
                for s in range(strips):
                    up = jnp.where(last_lane, ups[s + 1] if s + 1 < strips else walls, ups[s])
                    down = jnp.where(first_lane, downs[s - 1] if s else 0.0, downs[s])
                    total[s][c] = total[s][c] + (up + down)
            held = total
        before = None
        if first + count < planes:
            before = [axial(q, -1.0) for q in load(first + count - lo)]
        finish(count - 1, held, before)

    def arrive(h):
        for s in range(strips):
            in_copy(h, s).wait()
        edges(h)

    arrive(0)
    for h in range(chunks):
        if h + 1 < chunks:
            arrive(h + 1)

        @pl.loop(h * chunk_tiles, (h + 1) * chunk_tiles)
        def _(j):
            tile(j)

        out_copy(h).start()
    for h in range(chunks):
        out_copy(h).wait()


def main_call(first, count, angle_step, cycle, after, base=None):
    channels, planes, sector, cells = cycle.shape
    held = min(first + count + 1, planes) - max(first - 1, 0)
    anywhere = pl.BlockSpec(memory_space=pl.ANY)
    args = [in_hbm(cycle), after]
    if base is not None:
        args.append(base)
    tiles = sector // SUB
    chunks = 4 if tiles % 4 == 0 else 1
    return pl.pallas_call(
        functools.partial(main_kernel, first, count, angle_step),
        out_shape=jax.ShapeDtypeStruct(cycle.shape, f32),
        in_specs=[anywhere] * len(args),
        out_specs=anywhere,
        input_output_aliases={} if base is None else {2: 0},
        scratch_shapes=[
            pltpu.VMEM((channels, held, cells // LANES, sector, LANES), f32),
            pltpu.VMEM((channels, count, sector, cells), f32),
            pltpu.VMEM((count, channels, tiles + SUB, cells), f32),
            pltpu.VMEM((count, channels, tiles + SUB, cells), f32),
            pltpu.SemaphoreType.DMA((chunks, cells // LANES)),
            pltpu.SemaphoreType.DMA((chunks,)),
        ],
        compiler_params=pltpu.CompilerParams(vmem_limit_bytes=GRANT),
        name="cycle_planes_%d" % first,
    )(*args)


def pick(total, values, lanes, weights):
    for k in range(lanes.shape[0]):
        index = jnp.broadcast_to(lanes[k : k + 1], values.shape)
        term = jnp.take_along_axis(values, index, axis=1, mode="promise_in_bounds") * weights[k : k + 1]
        total = term if total is None else total + term
    return total


def norm_rows(weights):
    total = weights[0:1]
    for k in range(1, weights.shape[0]):
        total = total + weights[k : k + 1]
    return weights / total


def angles_of(own, sector, count):
    lane = lax.broadcasted_iota(jnp.int32, (1, sector), 1) + own * sector
    angle = (lane.astype(f32) + 0.5) * (2.0 * math.pi / count)
    return jnp.cos(angle), jnp.sin(angle)


DEEP = 4
SLOT = 32


def outgoing_kernel(ring, cycle, core, taps, raw_weights, far_ref, near_ref, odd_ref, send_ref, keep_ref,
                    core_ref, taps_ref, weights_ref, strip_ref, cycle_rows, side_ref, turn_ref, ends_ref, lane_ref, weight_ref, share_ref, sems):
    channels, planes, sector, cells = cycle.shape
    core_rows, core_cells = core_ref.shape[2:]
    lead = channels * planes
    own = lax.axis_index("azim")
    parity = lax.rem(own, 2)
    ring_even = parity == 0
    near = jnp.where(lax.rem(lax.axis_index("axial"), 2) == 0, planes - 1, 0)
    far = planes - 1 - near
    lane = lax.broadcasted_iota(jnp.int32, (1, LANES), 1)
    per = LANES // DEEP
    strip = pltpu.make_async_copy(cycle.at[:, :, :, pl.ds(0, LANES)], strip_ref, sems.at[4])
    copies = [
        pltpu.make_async_copy(cycle.at[:, :, pl.ds(0, SUB)], cycle_rows.at[0], sems.at[0]),
        pltpu.make_async_copy(cycle.at[:, :, pl.ds(sector - SUB, SUB)], cycle_rows.at[1], sems.at[1]),
        pltpu.make_async_copy(cycle.at[:, far], far_ref.at[:, pl.ds(0, sector)], sems.at[2]),
        pltpu.make_async_copy(cycle.at[:, near], near_ref.at[:, pl.ds(0, sector)], sems.at[3]),
    ]
    early = [
        pltpu.make_async_copy(core, core_ref, sems.at[5]),
        pltpu.make_async_copy(taps, taps_ref, sems.at[6]),
        pltpu.make_async_copy(raw_weights, weights_ref, sems.at[7]),
    ]
    for copy in early:
        copy.start()
    strip.start()
    for copy in copies:
        copy.start()
    groups = ring // 2
    for copy in early:
        copy.wait()

    sides = []
    side_ref[...] = jnp.zeros_like(side_ref)
    strips = -(-core_cells // LANES)
    width = core_cells - (strips - 1) * LANES
    for side in range(2):
        start = 0 if side == 0 else (strips - 1) * LANES
        at = 0 if side == 0 else width - DEEP
        for part in range(-(-lead // per)):
            total = None
            for i in range(part * per, min(lead, (part + 1) * per)):
                block = core_ref[i // planes, i % planes, :, start : min(start + LANES, core_cells)]
                if block.shape[1] < LANES:
                    block = jnp.concatenate(
                        [block, jnp.zeros((core_rows, LANES - block.shape[1]), f32)], axis=1
                    )
                turn = (DEEP * (i - part * per) - at) % LANES
                moved = pltpu.roll(block, turn, 1) if turn else block
                total = moved if total is None else jnp.where(lane // DEEP == i - part * per, moved, total)
            side_ref[0:core_rows, :] = total
            turn_ref[part * LANES : (part + 1) * LANES, 0:SLOT] = jnp.transpose(side_ref[...])
        total = turn_ref[pl.ds(0, lead, stride=DEEP), :]
        for d in range(1, DEEP):
            moved = pltpu.roll(turn_ref[pl.ds(d, lead, stride=DEEP), :], d * SLOT, 1)
            total = jnp.where(lane // SLOT == d, moved, total)
        sides.append(jnp.where(lane < DEEP * SLOT, total, 0.0))

    weights = norm_rows(weights_ref[...])
    cell = taps_ref[...]
    row = ((cell.astype(f32) + 0.5) * (1.0 / core_cells)).astype(jnp.int32)
    column = cell - row * core_cells
    row = row - own * core_rows
    here = (row >= 0) & (row < core_rows)
    left = here & (column < DEEP)
    right = here & (column >= core_cells - DEEP)
    depth = jnp.where(column < DEEP, column, column - (core_cells - DEEP))
    lane_ref[0] = jnp.where(left | right, depth * SLOT + row, 0)
    weight_ref[0] = jnp.where(left, weights, 0.0)
    weight_ref[1] = jnp.where(right, weights, 0.0)

    @pl.loop(0, ring)
    def _(s):
        part = pl.ds(pl.multiple_of(s * sector, sector), sector)
        lanes = lane_ref[0, :, part]
        total = pick(None, sides[0], lanes, weight_ref[0, :, part])
        share_ref[:, part] = pick(total, sides[1], lanes, weight_ref[1, :, part])

    whole = (strips - 1) * DEEP
    pairs = ends_ref.shape[0] - whole
    fold = DEEP // pairs

    @pl.when((own == 0) | (own == ring - 1))
    def _():
        base = jnp.where(own == 0, 0, core_rows - DEEP)
        if fold * width < LANES:
            ends_ref[...] = jnp.zeros_like(ends_ref)
        for i in range(lead):
            plane = core_ref[i // planes, i % planes]
            rows = jnp.where(own == 0, plane[:DEEP], plane[core_rows - DEEP :])
            for d in range(DEEP):
                for s in range(strips - 1):
                    ends_ref[s * DEEP + d, i : i + 1, :] = rows[d : d + 1, s * LANES : (s + 1) * LANES]
                at = (d % fold) * width
                ends_ref[whole + d // fold, i : i + 1, at : at + width] = rows[d : d + 1, (strips - 1) * LANES :]
        inside = here & (column >= DEEP) & (column < core_cells - DEEP)
        depth = row - base
        inside = inside & (depth >= 0) & (depth < DEEP)
        tail = column >= (strips - 1) * LANES
        lane_ref[0] = jnp.where(
            inside, jnp.where(tail, column - (strips - 1) * LANES + (depth % fold) * width, column % LANES), 0
        )
        for d in range(DEEP):
            for s in range(strips - 1):
                strip = inside & (column >= s * LANES) & (column < (s + 1) * LANES) & (depth == d)
                weight_ref[s * DEEP + d] = jnp.where(strip, weights, 0.0)
        for d in range(pairs):
            strip = inside & tail & (depth >= d * fold) & (depth < (d + 1) * fold)
            weight_ref[whole + d] = jnp.where(strip, weights, 0.0)

        @pl.loop(0, ring)
        def _(s):
            part = pl.ds(pl.multiple_of(s * sector, sector), sector)
            lanes = lane_ref[0, :, part]
            total = share_ref[:, part]
            for d in range(whole + pairs):
                total = pick(total, ends_ref[d], lanes, weight_ref[d, :, part])
            share_ref[:, part] = total

    strip.wait()
    trace = None
    for i in range(lead):
        block = strip_ref[i // planes, i % planes]
        moved = pltpu.roll(block, i, 1) if i else block
        trace = moved if trace is None else jnp.where(lane == i, moved, trace)
    trace = jnp.transpose(trace)[:lead]
    cosine, sine = angles_of(own, sector, sector * ring)
    last = pl.ds(groups * sector, sector)
    azimuthal, radial = trace[2 * planes : 3 * planes], trace[3 * planes : 4 * planes]
    send_ref[0 : 2 * planes, last] = trace[0 : 2 * planes]
    send_ref[2 * planes : 3 * planes, last] = radial * cosine - azimuthal * sine
    send_ref[3 * planes : 4 * planes, last] = radial * sine + azimuthal * cosine
    send_ref[4 * planes :, last] = trace[4 * planes :]

    for g in range(groups):
        to = pl.ds(g * sector, sector)
        mine = pl.ds(pl.multiple_of((2 * g + parity) * sector, sector), sector)
        other = pl.ds(pl.multiple_of((2 * g + 1 - parity) * sector, sector), sector)
        keep_ref[:, to] = share_ref[:, mine]
        send_ref[:, to] = share_ref[:, other]

    for c in range(channels):
        near_ref[c, sector:, 0:core_cells] = core_ref[c, near]
        far_ref[c, sector:, 0:core_cells] = core_ref[c, far]
    for copy in copies:
        copy.wait()
    at = (groups + 1) * sector
    for c in range(channels):
        for x in range(planes):
            i = c * planes + x
            low = cycle_rows[0, c, x, 0:1, :]
            high = cycle_rows[1, c, x, SUB - 1 : SUB, :]
            send_ref[i : i + 1, at : at + cells] = jnp.where(ring_even, high, low)
            odd_ref[i : i + 1, 0:cells] = jnp.where(ring_even, low, high)
            low = core_ref[c, x, 0:1, :]
            high = core_ref[c, x, core_rows - 1 : core_rows, :]
            send_ref[i : i + 1, at + cells : at + cells + core_cells] = jnp.where(ring_even, high, low)
            odd_ref[i : i + 1, cells : cells + core_cells] = jnp.where(ring_even, low, high)


def outgoing_call(ring, cycle, core, taps, weights):
    channels, planes, sector, cells = cycle.shape
    core_rows, core_cells = core.shape[2:]
    lead = channels * planes
    groups = ring // 2
    strips = -(-core_cells // LANES)
    fold = 2 if 2 * (core_cells - (strips - 1) * LANES) <= LANES else 1
    slots = (strips - 1) * DEEP + DEEP // fold
    parts = -(-lead * DEEP // LANES)
    whole = pl.BlockSpec(memory_space=pltpu.VMEM)
    anywhere = pl.BlockSpec(memory_space=pl.ANY)
    edge = cells + strips * LANES
    plane = jax.ShapeDtypeStruct((channels, sector + core_rows, cells), f32)
    return pl.pallas_call(
        functools.partial(outgoing_kernel, ring),
        out_shape=(
            plane,
            plane,
            jax.ShapeDtypeStruct((lead, edge), f32),
            jax.ShapeDtypeStruct((lead, (groups + 1) * sector + edge), f32),
            jax.ShapeDtypeStruct((lead, groups * sector), f32),
        ),
        in_specs=[anywhere] * 4,
        out_specs=(whole,) * 5,
        scratch_shapes=[
            pltpu.VMEM(core.shape, f32),
            pltpu.VMEM(taps.shape, jnp.int32),
            pltpu.VMEM(weights.shape, f32),
            pltpu.VMEM((channels, planes, sector, LANES), f32),
            pltpu.VMEM((2, channels, planes, SUB, cells), f32),
            pltpu.VMEM((SLOT, LANES), f32),
            pltpu.VMEM((parts * LANES, LANES), f32),
            pltpu.VMEM((slots, lead, LANES), f32),
            pltpu.VMEM((1,) + taps.shape, jnp.int32),
            pltpu.VMEM((slots,) + taps.shape, f32),
            pltpu.VMEM((lead, ring * sector), f32),
            pltpu.SemaphoreType.DMA((8,)),
        ],
        compiler_params=pltpu.CompilerParams(vmem_limit_bytes=GRANT),
        name="outgoing",
    )(in_hbm(cycle), in_hbm(core), in_hbm(taps), in_hbm(weights))


def relay_kernel(groups, sent, kept, got, after, own_ref, *outs):
    sector = own_ref.shape[1] // 3
    own = lax.axis_index("azim")
    group = own // 2
    even = lax.rem(own, 2) == 0
    last = pl.ds(groups * sector, sector)
    mine, other = sent[:, last], got[:, last]
    first = jnp.where(even, mine, other)
    second = jnp.where(even, other, mine)
    for s in range(groups):
        to = own_ref if s == 0 else outs[s - 1]
        target = group ^ s
        part = pl.ds(pl.multiple_of(target * sector, sector), sector)
        to[:, 0:sector] = kept[:, part] + got[:, part]
        to[:, sector : 2 * sector] = first
        to[:, 2 * sector :] = second


def relay_call(ring, sector, sent, kept, got, after):
    groups = ring // 2
    whole = pl.BlockSpec(memory_space=pltpu.VMEM)
    block = jax.ShapeDtypeStruct((kept.shape[0], 3 * sector), f32)
    return pl.pallas_call(
        functools.partial(relay_kernel, groups),
        out_shape=(block,) * groups,
        in_specs=[whole] * 3 + [pl.BlockSpec(memory_space=pl.ANY)],
        out_specs=(whole,) * groups,
        compiler_params=pltpu.CompilerParams(vmem_limit_bytes=GRANT),
        name="ghost_relay",
    )(sent, kept, got, in_hbm(after))


def final_kernel(ring, core_ref, taps_ref, weights_ref, got_ref, odd_ref, near_ref, far_ref, partial, *rest):
    groups = ring // 2
    blocks = rest[:groups]
    (cycle_out, core_out, k_ref, next_ref, prev_ref, turn_ref, strip, wing, brim,
     in_sem, out_sem) = rest[groups:]
    channels, planes, sector, cells = cycle_out.shape
    core_rows, core_cells = core_ref.shape[2:]
    lead = channels * planes
    own = lax.axis_index("azim")
    group = own // 2
    ring_even = lax.rem(own, 2) == 0
    core_even = lax.rem(lax.axis_index("axial"), 2) == 0
    inner = pl.ds(0, LANES)
    outer = pl.ds(LANES, cells - LANES)
    middle = pl.ds(1, planes - 2)
    ends = (pl.ds(0, SUB), pl.ds(sector - SUB, SUB))

    def places(ref):
        found = [(ref.at[:, x, :, inner], strip.at[x]) for x in range(planes)]
        found += [(ref.at[:, x, :, outer], wing.at[n]) for n, x in enumerate((0, planes - 1))]
        found += [(ref.at[:, middle, ends[n], outer], brim.at[n]) for n in range(2)]
        return found

    def in_copies():
        return [
            pltpu.make_async_copy(a, b, in_sem.at[n]) for n, (a, b) in enumerate(places(partial))
        ]

    def out_copies():
        return [
            pltpu.make_async_copy(b, a, out_sem.at[n]) for n, (a, b) in enumerate(places(cycle_out))
        ]

    coming, leaving = in_copies(), out_copies()
    for copy in coming:
        copy.start()
    lane = lax.broadcasted_iota(jnp.int32, (1, LANES), 1)

    total = blocks[0][:, 0:sector]
    for s in range(1, groups):
        total = total + blocks[s][:, 0:sector]
    cosine, sine = angles_of(own, sector, sector * ring)
    q = [total[c * planes : (c + 1) * planes] for c in range(5)]
    q[2], q[3] = q[3] * cosine - q[2] * sine, q[2] * cosine + q[3] * sine
    u, pressure, enthalpy = velocities(q)
    inside = inner_radius - 0.5 * radial_step
    beta = RAD_BETA * inside / (inside + radial_step)
    _, after = to_sides(q, u, pressure, enthalpy, 3, RAD_ALPHA, beta)
    turn_ref[...] = jnp.zeros_like(turn_ref)
    for c in range(5):
        turn_ref[c * planes : (c + 1) * planes, :] = after[c]
    gift = jnp.transpose(turn_ref[...])

    taps, weights = taps_ref[...], norm_rows(weights_ref[...])
    ghosts = taps.shape[1]
    wide = 2 * LANES
    span = lax.broadcasted_iota(jnp.int32, (1, wide), 1)
    shift = own * core_rows
    side_end = jnp.where(own == 0, 2 * core_cells, 3 * core_cells)

    def targets(t):
        left = pltpu.roll(t, ghosts - shift, 1)[:, :wide]
        right = pltpu.roll(t, lax.rem(2 * ghosts + core_rows - core_cells - shift, ghosts), 1)[:, :wide]
        end = pltpu.roll(t, lax.rem(2 * ghosts + PAIR - side_end, ghosts), 1)[:, :wide]
        return jnp.where(span < core_rows, left, jnp.where(span < PAIR, right, end))

    taps, weights = targets(taps), targets(weights)
    lanes = taps % sector
    home = taps // sector
    found = [None, None]
    for s in range(groups):
        for y in range(2):
            values = blocks[s][:, (1 + y) * sector : (2 + y) * sector]
            masked = jnp.where(home == 2 * (group ^ s) + y, weights, 0.0)
            for h in range(2):
                part = slice(h * LANES, (h + 1) * LANES)
                found[h] = pick(found[h], values, lanes[:, part], masked[:, part])
    found = jnp.concatenate(found, axis=1)
    turn_ref[0:lead, :] = found[:, 0:LANES]
    sides = jnp.transpose(turn_ref[...])
    left_side = sides[0:core_rows]
    right_side = sides[core_rows : 2 * core_rows]
    found = found[:, PAIR : PAIR + core_cells]

    for x in range(planes):
        coming[x].wait()
        for c in range(5):
            i = c * planes + x
            moved = pltpu.roll(gift, (LANES - i) % LANES, 1)
            strip[x, c, :, :] += jnp.where(lane == 0, moved, 0.0)
    for copy in coming[planes:]:
        copy.wait()

    def sides(q):
        u, pressure, enthalpy = velocities(q)
        return to_sides(q, u, pressure, enthalpy, 1, AX_ALPHA, AX_BETA)

    @pl.loop(0, sector // SUB)
    def _(j):
        part = pl.ds(pl.multiple_of(j * SUB, SUB), SUB)
        near = [near_ref[c, part, :] for c in range(5)]
        far = [far_ref[c, part, :] for c in range(5)]
        _, low = sides([jnp.where(core_even, far[c], near[c]) for c in range(5)])
        high, _ = sides([jnp.where(core_even, near[c], far[c]) for c in range(5)])
        for n, value in enumerate((low, high)):
            for c in range(5):
                strip[n * (planes - 1), c, part, :] += value[c][:, :LANES]
                wing[n, c, part, :] += value[c][:, LANES:]

    _, radius_inv = radial_tables(cells)
    alpha2, beta2 = azim_coefs(radius_inv, 2.0 * math.pi / (sector * ring))
    def row_pair(start, width):
        pairs = []
        for c in range(5):
            odd = odd_ref[c * planes : (c + 1) * planes, start : start + width]
            even = got_ref[c * planes : (c + 1) * planes, edge + start : edge + start + width]
            pairs.append((jnp.where(ring_even, odd, even), jnp.where(ring_even, even, odd)))
        return [p[0] for p in pairs], [p[1] for p in pairs]

    edge = (groups + 1) * sector
    low, high = row_pair(0, cells)
    _, low = edge_rows(low, alpha2, beta2)
    high, _ = edge_rows(high, alpha2, beta2)
    for n, value in enumerate((low, high)):
        at = n * (sector - 1)
        small = n * (SUB - 1)
        for c in range(5):
            for x in range(planes):
                strip[x, c, at : at + 1, :] += value[c][x : x + 1, :LANES]
                rest_row = value[c][x : x + 1, LANES:]
                if 0 < x < planes - 1:
                    brim[n, c, x - 1, small : small + 1, :] += rest_row
                else:
                    wing[min(x, 1), c, at : at + 1, :] += rest_row
    for copy in leaving:
        copy.start()

    strips = k_ref.shape[2]
    padded = k_ref.shape[3]
    tail = strips * LANES - core_cells
    body = LANES - tail
    lows, highs = row_pair(cells, core_cells)
    for c in range(5):
        low, high = lows[c], highs[c]
        ends = found[c * planes : (c + 1) * planes]
        low = jnp.where(own == 0, ends, low)
        high = jnp.where(own == ring - 1, ends, high)
        for x in range(planes):
            i = c * planes + x
            for s in range(strips - 1):
                k_ref[c, x, s, 0:core_rows, :] = core_ref[c, x, :, s * LANES : (s + 1) * LANES]
            k_ref[c, x, strips - 1, 0:core_rows, 0:body] = core_ref[c, x, :, (strips - 1) * LANES :]
            pad = jnp.where(
                lane == LANES - 1,
                pltpu.roll(left_side, (LANES - 1 - i) % LANES, 1),
                pltpu.roll(right_side, (body - i) % LANES, 1),
            )
            k_ref[c, x, strips - 1, 0:core_rows, body:] = pad[:, body:]
            for row, value in ((core_rows, high), (padded - 1, low)):
                for s in range(strips - 1):
                    k_ref[c, x, s, row : row + 1, :] = value[x : x + 1, s * LANES : (s + 1) * LANES]
                k_ref[c, x, strips - 1, row : row + 1, 0:body] = value[x : x + 1, (strips - 1) * LANES :]

    def load(c, x, part):
        return jnp.concatenate([k_ref[c, x, s, part, :] for s in range(strips)], axis=1)

    tiles = padded // SUB
    for x in range(planes):
        start = [load(c, x, pl.ds(0, tiles, stride=SUB)) for c in range(5)]
        before, _ = edge_rows(start, CORE_ALPHA, CORE_BETA)
        end = [load(c, x, pl.ds(SUB - 1, tiles, stride=SUB)) for c in range(5)]
        _, after = edge_rows(end, CORE_ALPHA, CORE_BETA)
        for c in range(5):
            next_ref[x, c, 0:tiles, :] = before[c]
            prev_ref[x, c, SUB : SUB + tiles, :] = after[c]
            prev_ref[x, c, SUB - 1 : SUB, :] = after[c][tiles - 1 : tiles]

    row = lax.broadcasted_iota(jnp.int32, (SUB, 1), 0)
    center = 1.0 - 2.0 * AX_ALPHA - 4.0 * CORE_ALPHA
    full = strips * LANES
    for j in range(-(-core_rows // SUB)):
        size = min(SUB, core_rows - j * SUB)
        part = pl.ds(j * SUB, SUB)
        here = pl.ds(j * SUB, size)

        def outside(ref):
            q = [ref[c, pl.ds(sector + j * SUB, size), 0:core_cells] for c in range(5)]
            u, pressure, enthalpy = velocities(q)
            return to_sides(q, u, pressure, enthalpy, 1, AX_ALPHA, AX_BETA)

        near_before, near_after = outside(near_ref)
        far_before, far_after = outside(far_ref)
        from_low = [jnp.where(core_even, a, b) for a, b in zip(far_after, near_after)]
        from_high = [jnp.where(core_even, a, b) for a, b in zip(near_before, far_before)]
        carry, held = None, None
        for x in range(planes):
            q = [load(c, x, part) for c in range(5)]
            u, pressure, enthalpy = velocities(q)
            before, after = to_sides(q, u, pressure, enthalpy, 1, AX_ALPHA, AX_BETA)
            if held is not None:
                for c in range(5):
                    core_out[c, x - 1, here, :] = (held[c] + before[c])[:size, :core_cells]
            result = [q[c] * center for c in range(5)]
            if carry is not None:
                result = [result[c] + carry[c] for c in range(5)]
            carry = after
            before, after = to_sides(q, u, pressure, enthalpy, 2, CORE_ALPHA, CORE_BETA)
            for c in range(5):
                above = next_ref[x, c, pl.ds((j + 1) % tiles, 1), :]
                below = prev_ref[x, c, pl.ds(j + SUB - 1, 1), :]
                up = pltpu.roll(before[c], SUB - 1, 0)
                down = pltpu.roll(after[c], 1, 0)
                result[c] = result[c] + (
                    jnp.where(row == SUB - 1, above, up) + jnp.where(row == 0, below, down)
                )
            before, after = to_sides(q, u, pressure, enthalpy, 3, CORE_ALPHA, CORE_BETA)
            for c in range(5):
                result[c] = result[c] + (
                    pltpu.roll(before[c], full - 1, 1) + pltpu.roll(after[c], 1, 1)
                )
            held = result
        for c in range(5):
            core_out[c, planes - 1, here, :] = held[c][:size, :core_cells] + from_high[c]
            core_out[c, 0, here, :] += from_low[c]

    for copy in leaving:
        copy.wait()


def final_call(ring, core, taps, weights, got, odd, near, far, partial, blocks):
    channels, planes, sector, cells = partial.shape
    core_rows, core_cells = core.shape[2:]
    strips = -(-(core_cells + 2) // LANES)
    padded = -(-(core_rows + 2) // SUB) * SUB
    whole = pl.BlockSpec(memory_space=pltpu.VMEM)
    anywhere = pl.BlockSpec(memory_space=pltpu.HBM)
    groups = ring // 2
    edge_shape = (planes, channels, 2 * SUB, strips * LANES)
    return pl.pallas_call(
        functools.partial(final_kernel, ring),
        out_shape=(
            jax.ShapeDtypeStruct(partial.shape, f32),
            jax.ShapeDtypeStruct(core.shape, f32),
        ),
        in_specs=[whole] * 7 + [anywhere] + [whole] * groups,
        out_specs=(anywhere, whole),
        input_output_aliases={7: 0},
        scratch_shapes=[
            pltpu.VMEM((channels, planes, strips, padded, LANES), f32),
            pltpu.VMEM(edge_shape, f32),
            pltpu.VMEM(edge_shape, f32),
            pltpu.VMEM((LANES, LANES), f32),
            pltpu.VMEM((planes, channels, sector, LANES), f32),
            pltpu.VMEM((2, channels, sector, cells - LANES), f32),
            pltpu.VMEM((2, channels, planes - 2, SUB, cells - LANES), f32),
            pltpu.SemaphoreType.DMA((planes + 4,)),
            pltpu.SemaphoreType.DMA((planes + 4,)),
        ],
        compiler_params=pltpu.CompilerParams(vmem_limit_bytes=GRANT),
        name="late_terms",
    )(core, taps, weights, got, odd, near, far, partial, *blocks)


def body(cycle, core, core_taps, core_weights, cycle_taps, cycle_weights):
    planes, sector = cycle.shape[1:3]
    ring = lax.axis_size("azim")
    length = lax.axis_size("axial")
    angle_step = 2.0 * math.pi / (sector * ring)
    even_axial = [(i, i ^ 1) for i in range(length)]
    odd_axial = [(i, (i + 1) % length) for i in range(1, length, 2)]
    odd_axial += [(b, a) for a, b in odd_axial]
    even_azim = [(i, i ^ 1) for i in range(ring)]
    odd_azim = [(i, (i + 1) % ring) for i in range(1, ring, 2)]
    odd_azim += [(b, a) for a, b in odd_azim]
    far, near, odd, sent, kept = outgoing_call(ring, cycle, core, cycle_taps.T, cycle_weights.T)
    got = lax.ppermute(sent, "azim", even_azim)
    far = lax.ppermute(far, "axial", odd_axial)
    near = lax.ppermute(near, "axial", even_axial)
    odd = lax.ppermute(odd, "azim", odd_azim)
    half = planes // 2
    partial = main_call(0, half, angle_step, cycle, kept)
    blocks = list(relay_call(ring, sector, sent, kept, got, partial))
    partial = main_call(half, planes - half, angle_step, cycle, blocks[0], partial)
    for s in range(1, ring // 2):
        blocks[s] = lax.ppermute(blocks[s], "azim", [(i, i ^ (2 * s)) for i in range(ring)])
    return tuple(
        final_call(ring, core, core_taps.T, core_weights.T, got, odd, near, far, partial, blocks)
    )


def solution(mesh):
    placed = (P(None, "axial", "azim", None), P(None, "axial", "azim", None), P(), P(), P(), P())
    return jax.shard_map(
        body,
        mesh=mesh,
        in_specs=placed,
        out_specs=(P(None, "axial", "azim", None), P(None, "axial", "azim", None)),
        check_vma=False,
    )
```

time: 202 us -> 37.6 us (0.19)
  other arithmetic: 63.6 us -> 0 us
  local copies, waits for them, and re-layouts: 35 us -> 0.01 us
  blocking collectives: 30.6 us -> 0 us
  Pallas kernels: 0 us -> 24.5 us
  waiting for transfers between devices: 22.6 us -> 0.02 us
  matrix products: 21.8 us -> 0 us
  between operations: 14.6 us -> 0.74 us
    all_gather x1 -> x0, blocking collectives: 30.6 us -> none  [body(): all_traces = lax.all_gather(cart_trace, 'azim', axis=2, tiled=True)]
    add x3 -> x0, other arithmetic: 29.2 us -> none  [the longest x1 25.5 us: body(): cycle_state + time_step * cycle_rhs(padded, inner_ghost, angle_step)]
    pallas_call x0 -> x5, Pallas kernels: none -> 24.5 us  [the longest x2 12.3 us: main_call(): pl.pallas_call(functools.partial(main_kernel, first, count, angle_step),...]
    dot_general x2 -> x0, matrix products: 21.8 us -> none  [apply_taps(): jnp.dot(flat_values, matrix, preferred_element_type=jnp.float32, precisio...]
    reduce_scatter x1 -> x0, waiting for transfers between devices: 21.7 us -> none  [body(): lax.psum_scatter(cycle_share, 'azim', scatter_dimension=2, tiled=True)]
    unnamed x60 -> x6, local copies, waits for them, and re-layouts: 19.5 us -> 0.01 us
    unnamed x22 -> x0, other arithmetic: 8.84 us -> none
    concatenate x4 -> x0, other arithmetic: 7.91 us -> none  [the longest x1 6.04 us: cycle_rhs(): jnp.concatenate([inner_ghost[..., None], center, outer_ghost[..., None]],...]
  transfers between devices with their start and end apart: 9 -> 7, of which waited for: 2 -> 0; matrix products, arithmetic and copies ran while one was open for 29% -> 0% of each run, Pallas kernels for 0% -> 33%
where the time goes in v1:
time: 37.6 us; the launch traced here: 37.4 us
  Pallas kernels  24.5 us (65%)
  starting transfers between devices  12.1 us (32%)
  between operations  0.74 us (2%)
    pallas_call x2, Pallas kernels, main_call(): pl.pallas_call(functools.partial(main_kernel, first, count, angle_step),...  12.3 us
    pallas_call x1, Pallas kernels, outgoing_call(): pl.pallas_call(functools.partial(outgoing_kernel, ring), out_shape=(plane...  6.45 us
    pallas_call x1, Pallas kernels, final_call(): pl.pallas_call(functools.partial(final_kernel, ring), out_shape=(jax.Shap...  5.75 us
    ppermute x1, starting transfers between devices, body(): odd = lax.ppermute(odd, 'azim', odd_azim)  4.56 us
    ppermute x3, starting transfers between devices, body(): lax.ppermute(blocks[s], 'azim', [(i, i ^ 2 * s) for i in range(ring)])  4.45 us
    ppermute x1, starting transfers between devices, body(): far = lax.ppermute(far, 'axial', odd_axial)  2.61 us
  transfers between devices with their start and end apart: 7, of which 0 were waited for; matrix products, arithmetic and copies ran while one was open for 0% of the time, Pallas kernels for 33%

profile of v1, /device:TPU:0, one launch (start us, length us, event | category | flops | bytes accessed | tf_op | source)
XLA Modules:
  0.0 37.4 jit_solution(17376727765639985298)
XLA Ops:
  0.6 6.5 %outgoing.1 = (f32[5,152,256]{2,1,0:T(8,128)S(1)}, f32[5,152,256]{2,1,0:T(8,128)S(1)}, f32[40,512]{1,0:T(8,128)S(1)}, f32[40,1152]{1,0:T(8,128)S(1)}, f32[40,512]{1,0:T(8,128)S(1)}) custom-call(f32[5,8,128,256]{3,2,1,0:T(8,128)} %q_hbm.3, f32[5,8,24,192]{3,2,1,0:T(8,128)} %core_ref.1, s32[4,1024]{1,0:T(4,128)} %bitcast.6, f32[4,1024]{1,0:T(4,128)} %bitcast.7), custom_call_target="tpu_custom_call" | custom-call | tf_op jit(solution)/shard_map/outgoing/pallas_call | solution.py:481
  7.1 0.5 %collective-permute-start.2 = (f32[5,152,256]{2,1,0:T(8,128)S(1)}, f32[5,152,256]{2,1,0:T(8,128)S(1)}, u32[]{:S(2)}, u32[]{:S(2)}) collective-permute-start(f32[5,152,256]{2,1,0:T(8,128)S(1)} %get-tuple-element.13), channel_id=1, source_target_pairs={{0,8},{8,0},{16,24},{24,16},{1,9},{9,1},{17,25},{25,17},{2,10},{10... | collective-permute-start | bytes 2334728 | tf_op jit(solution)/shard_map/ppermute | solution.py:820
  7.6 2.6 %collective-permute-start.3 = (f32[5,152,256]{2,1,0:T(8,128)S(1)}, f32[5,152,256]{2,1,0:T(8,128)S(1)}, u32[]{:S(2)}, u32[]{:S(2)}) collective-permute-start(f32[5,152,256]{2,1,0:T(8,128)S(1)} %get-tuple-element.14), channel_id=1, source_target_pairs={{8,16},{24,0},{16,8},{0,24},{9,17},{25,1},{17,9},{1,25},{10,18},{2... | collective-permute-start | bytes 2334728 | tf_op jit(solution)/shard_map/ppermute | solution.py:819
  10.2 0.0 collective-permute-start
  10.2 4.6 %collective-permute-start.1 = (f32[40,512]{1,0:T(8,128)S(1)}, f32[40,512]{1,0:T(8,128)S(1)}, u32[]{:S(2)}, u32[]{:S(2)}) collective-permute-start(f32[40,512]{1,0:T(8,128)S(1)} %get-tuple-element.12), channel_id=1, source_target_pairs={{1,2},{3,4},{5,6},{7,0},{2,1},{4,3},{6,5},{0,7},{9,10},{11,12},{13... | collective-permute-start | bytes 245768 | tf_op jit(solution)/shard_map/ppermute | solution.py:821
  14.8 6.1 %cycle_planes_0.1.after.rest_1_ = f32[5,8,128,256]{3,2,1,0:T(8,128)} custom-call(f32[5,8,128,256]{3,2,1,0:T(8,128)} %q_hbm.3, f32[40,512]{1,0:T(8,128)S(1)} %get-tuple-element.15.rest_0_.kept), custom_call_target="tpu_custom_call" | custom-call | tf_op jit(solution)/shard_map/cycle_planes_0/pallas_call | solution.py:263
  20.9 0.0 collective-permute-done.got.got_ref
  21.0 0.1 collective-permute-start.4
  21.0 1.6 %collective-permute-start.5 = (f32[40,384]{1,0:T(8,128)S(1)}, f32[40,384]{1,0:T(8,128)S(1)}, u32[]{:S(2)}, u32[]{:S(2)}) collective-permute-start(f32[40,384]{1,0:T(8,128)S(1)} %get-tuple-element.18), channel_id=1, source_target_pairs={{0,4},{1,5},{2,6},{3,7},{4,0},{5,1},{6,2},{7,3},{8,12},{9,13},{10,... | collective-permute-start | bytes 184328 | tf_op jit(solution)/shard_map/ppermute | solution.py:827
  22.6 0.0 collective-permute-done.1.odd_ref
  22.6 2.8 %collective-permute-start.6 = (f32[40,384]{1,0:T(8,128)S(1)}, f32[40,384]{1,0:T(8,128)S(1)}, u32[]{:S(2)}, u32[]{:S(2)}) collective-permute-start(f32[40,384]{1,0:T(8,128)S(1)} %get-tuple-element.19), channel_id=1, source_target_pairs={{0,6},{1,7},{2,4},{3,5},{4,2},{5,3},{6,0},{7,1},{8,14},{9,15},{10,... | collective-permute-start | bytes 184328 | tf_op jit(solution)/shard_map/ppermute | solution.py:827
  25.4 0.0 copy-start
  25.4 0.0 copy-start.1
  25.4 0.0 copy-start.2
  25.4 6.2 %cycle_planes_4.1.partial = f32[5,8,128,256]{3,2,1,0:T(8,128)} custom-call(f32[5,8,128,256]{3,2,1,0:T(8,128)} %q_hbm.3, f32[40,384]{1,0:T(8,128)S(1)} %get-tuple-element.16.rest_0_, f32[5,8,128,256]{3,2,1,0:T(8,128)} %cycle_planes_0.1.after.rest_1_), custom_call_target="tpu_custom_call", output_to_operand_aliasing={{}: (2, {})} | custom-call | tf_op jit(solution)/shard_map/cycle_planes_4/pallas_call | solution.py:263
  31.6 0.0 collective-permute-done.4.rest_1_
  31.6 0.0 collective-permute-done.5.rest_2_
  31.6 0.0 collective-permute-done.6.rest_3_
  31.6 0.0 collective-permute-done.2.near_ref
  31.7 0.0 collective-permute-done.3.far_ref
  31.7 0.0 copy-done
  31.7 0.0 copy-done.1
  31.7 0.0 copy-done.2
  31.7 5.7 %late_terms.1 = (f32[5,8,128,256]{3,2,1,0:T(8,128)}, f32[5,8,24,192]{3,2,1,0:T(8,128)}) custom-call(f32[5,8,24,192]{3,2,1,0:T(8,128)S(1)} %copy-done, s32[4,768]{1,0:T(4,128)S(1)} %bitcast.4, f32[4,768]{1,0:T(4,128)S(1)} %bitcast.5, f32[40,1152]{1,0:T(8,128)S(1)} %collective-permute-done.got.got_ref, ...), custom_call_target="tpu_custom_call", output_to_operand_aliasing={{0}: (7, {})} | custom-call | tf_op jit(solution)/shard_map/late_terms/pallas_call | solution.py:781
  (1 shorter events, 0.0 us)
Async XLA Ops:
  7.1 24.6 %collective-permute-start.2 = (f32[5,152,256]{2,1,0:T(8,128)S(1)}, f32[5,152,256]{2,1,0:T(8,128)S(1)}, u32[]{:S(2)}, u32[]{:S(2)}) collective-permute-start(f32[5,152,256]{2,1,0:T(8,128)S(1)} %get-tuple-element.13), channel_id=1, source_target_pairs={{0,8},{8,0},{16,24},{24,16},{1,9},{9,1},{17,25},{25,17},{2,10},{10... | collective-permute-start | bytes 2334728 | tf_op jit(solution)/shard_map/ppermute | solution.py:820
  7.6 24.1 %collective-permute-start.3 = (f32[5,152,256]{2,1,0:T(8,128)S(1)}, f32[5,152,256]{2,1,0:T(8,128)S(1)}, u32[]{:S(2)}, u32[]{:S(2)}) collective-permute-start(f32[5,152,256]{2,1,0:T(8,128)S(1)} %get-tuple-element.14), channel_id=1, source_target_pairs={{8,16},{24,0},{16,8},{0,24},{9,17},{25,1},{17,9},{1,25},{10,18},{2... | collective-permute-start | bytes 2334728 | tf_op jit(solution)/shard_map/ppermute | solution.py:819
  10.2 10.7 %collective-permute-start = (f32[40,1152]{1,0:T(8,128)S(1)}, f32[40,1152]{1,0:T(8,128)S(1)}, u32[]{:S(2)}, u32[]{:S(2)}) collective-permute-start(f32[40,1152]{1,0:T(8,128)S(1)} %get-tuple-element.11.sent), channel_id=1, source_target_pairs={{0,1},{1,0},{2,3},{3,2},{4,5},{5,4},{6,7},{7,6},{8,9},{9,8},{10,11... | collective-permute-start | bytes 552968 | tf_op jit(solution)/shard_map/ppermute | solution.py:818
  10.2 12.4 %collective-permute-start.1 = (f32[40,512]{1,0:T(8,128)S(1)}, f32[40,512]{1,0:T(8,128)S(1)}, u32[]{:S(2)}, u32[]{:S(2)}) collective-permute-start(f32[40,512]{1,0:T(8,128)S(1)} %get-tuple-element.12), channel_id=1, source_target_pairs={{1,2},{3,4},{5,6},{7,0},{2,1},{4,3},{6,5},{0,7},{9,10},{11,12},{13... | collective-permute-start | bytes 245768 | tf_op jit(solution)/shard_map/ppermute | solution.py:821
  21.0 10.7 %collective-permute-start.4 = (f32[40,384]{1,0:T(8,128)S(1)}, f32[40,384]{1,0:T(8,128)S(1)}, u32[]{:S(2)}, u32[]{:S(2)}) collective-permute-start(f32[40,384]{1,0:T(8,128)S(1)} %get-tuple-element.17), channel_id=1, source_target_pairs={{0,2},{1,3},{2,0},{3,1},{4,6},{5,7},{6,4},{7,5},{8,10},{9,11},{10,... | collective-permute-start | bytes 184328 | tf_op jit(solution)/shard_map/ppermute | solution.py:827
  21.0 10.6 %collective-permute-start.5 = (f32[40,384]{1,0:T(8,128)S(1)}, f32[40,384]{1,0:T(8,128)S(1)}, u32[]{:S(2)}, u32[]{:S(2)}) collective-permute-start(f32[40,384]{1,0:T(8,128)S(1)} %get-tuple-element.18), channel_id=1, source_target_pairs={{0,4},{1,5},{2,6},{3,7},{4,0},{5,1},{6,2},{7,3},{8,12},{9,13},{10,... | collective-permute-start | bytes 184328 | tf_op jit(solution)/shard_map/ppermute | solution.py:827
  22.6 9.0 %collective-permute-start.6 = (f32[40,384]{1,0:T(8,128)S(1)}, f32[40,384]{1,0:T(8,128)S(1)}, u32[]{:S(2)}, u32[]{:S(2)}) collective-permute-start(f32[40,384]{1,0:T(8,128)S(1)} %get-tuple-element.19), channel_id=1, source_target_pairs={{0,6},{1,7},{2,4},{3,5},{4,2},{5,3},{6,0},{7,1},{8,14},{9,15},{10,... | collective-permute-start | bytes 184328 | tf_op jit(solution)/shard_map/ppermute | solution.py:827
  25.4 6.3 %copy-start = (f32[5,8,24,192]{3,2,1,0:T(8,128)S(1)}, f32[5,8,24,192]{3,2,1,0:T(8,128)}, u32[]{:S(2)}) copy-start(f32[5,8,24,192]{3,2,1,0:T(8,128)} %core_ref.1) | copy-start | bytes 2211844
  25.4 6.3 %copy-start.1 = (s32[768,4]{0,1:T(4,128)S(1)}, s32[768,4]{0,1:T(4,128)}, u32[]{:S(2)}) copy-start(s32[768,4]{0,1:T(4,128)} %param.8) | copy-start | bytes 36868
  25.4 6.3 %copy-start.2 = (f32[768,4]{0,1:T(4,128)S(1)}, f32[768,4]{0,1:T(4,128)}, u32[]{:S(2)}) copy-start(f32[768,4]{0,1:T(4,128)} %param.9) | copy-start | bytes 36868

commit v2 on v1

--- a/solution.py
+++ b/solution.py
@@ -19,11 +19,15 @@
 LANES = 128
 SUB = 8
 PAIR = 64
-GRANT = 40 * 1024 * 1024
+GRANT = 16 * 1024 * 1024
 
 
 def in_hbm(x):
     return pltpu.with_memory_space_constraint(x, pltpu.HBM)
+
+
+def in_vmem(x):
+    return pltpu.with_memory_space_constraint(x, pltpu.VMEM)
 f32 = jnp.float32
 AX_ALPHA = time_step * viscosity / (axial_step * axial_step)
 AX_BETA = time_step / (2.0 * axial_step)
@@ -88,33 +92,12 @@
     )
 
 
-def main_kernel(first, count, angle_step, q_hbm, *rest):
-    out_hbm, q_ref, out_ref, next_ref, prev_ref, in_sem, out_sem = rest[-7:]
-    planes = q_hbm.shape[1]
-    sector, cells = q_hbm.shape[2], q_hbm.shape[3]
-    chunks = in_sem.shape[0]
-    rows = sector // chunks
-    lo = max(first - 1, 0)
-    hi = min(first + count + 1, planes)
-    strips = cells // LANES
-
-    def in_copy(h, s):
-        part = pl.ds(h * rows, rows)
-        return pltpu.make_async_copy(
-            q_hbm.at[:, pl.ds(lo, hi - lo), part, pl.ds(s * LANES, LANES)],
-            q_ref.at[:, :, s, part],
-            in_sem.at[h, s],
-        )
-
-    def out_copy(h):
-        part = pl.ds(h * rows, rows)
-        return pltpu.make_async_copy(
-            out_ref.at[:, :, part], out_hbm.at[:, pl.ds(first, count), part], out_sem.at[h]
-        )
-
-    for h in range(chunks):
-        for s in range(strips):
-            in_copy(h, s).start()
+def main_kernel(first, count, angle_step, q_ref, after, *rest):
+    out_ref, next_ref, prev_ref = rest[0], rest[-2], rest[-1]
+    if len(rest) > 3:
+        rest[1][...] = after[...]
+    planes, strips, sector = q_ref.shape[1:4]
+    cells = strips * LANES
     unit = 1.0 / AX_BETA
     lane = lax.broadcasted_iota(jnp.int32, (1, LANES), 1)
     first_lane = lane == 0
@@ -139,29 +122,23 @@
     radial_alpha = RAD_ALPHA * unit
 
     tiles = sector // SUB
-    chunk_tiles = tiles // chunks
     zero = jnp.zeros((1, cells), f32)
     for i in range(count):
         for c in range(5):
             prev_ref[i, c, SUB - 1 : SUB, :] = zero
             next_ref[i, c, tiles : tiles + 1, :] = zero
 
-    def edges(h):
-        for i in range(count):
-            x = first + i - lo
-            for s in range(strips):
-                alpha2, beta2 = coefs[s][0][:chunk_tiles], coefs[s][1][:chunk_tiles]
-                wide = slice(s * LANES, (s + 1) * LANES)
-                q = [q_ref[c, x, s, pl.ds(h * rows, chunk_tiles, stride=SUB), :] for c in range(5)]
-                before, _ = edge_rows(q, alpha2, beta2)
-                q = [
-                    q_ref[c, x, s, pl.ds(h * rows + SUB - 1, chunk_tiles, stride=SUB), :]
-                    for c in range(5)
-                ]
-                _, after = edge_rows(q, alpha2, beta2)
-                for c in range(5):
-                    next_ref[i, c, pl.ds(h * chunk_tiles, chunk_tiles), wide] = before[c]
-                    prev_ref[i, c, pl.ds(SUB + h * chunk_tiles, chunk_tiles), wide] = after[c]
+    for i in range(count):
+        for s in range(strips):
+            alpha2, beta2 = coefs[s][0][:1], coefs[s][1][:1]
+            wide = slice(s * LANES, (s + 1) * LANES)
+            q = [q_ref[c, first + i, s, pl.ds(0, tiles, stride=SUB), :] for c in range(5)]
+            before, _ = edge_rows(q, alpha2, beta2)
+            q = [q_ref[c, first + i, s, pl.ds(SUB - 1, tiles, stride=SUB), :] for c in range(5)]
+            _, after = edge_rows(q, alpha2, beta2)
+            for c in range(5):
+                next_ref[i, c, 0:tiles, wide] = before[c]
+                prev_ref[i, c, SUB : SUB + tiles, wide] = after[c]
 
     def straight(q):
         return q if abs(ratio - 1.0) < 1e-9 else q * ratio
@@ -182,10 +159,10 @@
                     value = held[s][c] if before is None else held[s][c] + before[s][c]
                     out_ref[c, i, part, s * LANES : (s + 1) * LANES] = value * AX_BETA
 
-        carry = [axial(q, 1.0) for q in load(0)] if first > 0 else None
+        carry = [axial(q, 1.0) for q in load(first - 1)] if first > 0 else None
         held = None
         for i in range(count):
-            q = load(first + i - lo)
+            q = load(first + i)
             flux = [all_fluxes(q[s]) for s in range(strips)]
             if held is not None:
                 finish(
@@ -229,54 +206,31 @@
             held = total
         before = None
         if first + count < planes:
-            before = [axial(q, -1.0) for q in load(first + count - lo)]
+            before = [axial(q, -1.0) for q in load(first + count)]
         finish(count - 1, held, before)
 
-    def arrive(h):
-        for s in range(strips):
-            in_copy(h, s).wait()
-        edges(h)
-
-    arrive(0)
-    for h in range(chunks):
-        if h + 1 < chunks:
-            arrive(h + 1)
-
-        @pl.loop(h * chunk_tiles, (h + 1) * chunk_tiles)
-        def _(j):
-            tile(j)
-
-        out_copy(h).start()
-    for h in range(chunks):
-        out_copy(h).wait()
-
-
-def main_call(first, count, angle_step, cycle, after, base=None):
-    channels, planes, sector, cells = cycle.shape
-    held = min(first + count + 1, planes) - max(first - 1, 0)
-    anywhere = pl.BlockSpec(memory_space=pl.ANY)
-    args = [in_hbm(cycle), after]
-    if base is not None:
-        args.append(base)
-    tiles = sector // SUB
-    chunks = 4 if tiles % 4 == 0 else 1
+    @pl.loop(0, tiles)
+    def _(j):
+        tile(j)
+
+
+def main_call(first, count, angle_step, held, after, handed_on):
+    channels, planes, strips, sector = held.shape[:4]
+    cells = strips * LANES
+    whole = pl.BlockSpec(memory_space=pltpu.VMEM)
+    edge = (count, channels, sector // SUB + SUB, cells)
+    shapes = [pltpu.VMEM((channels, count, sector, cells), f32)]
+    if handed_on:
+        shapes.append(jax.ShapeDtypeStruct(after.shape, f32))
     return pl.pallas_call(
         functools.partial(main_kernel, first, count, angle_step),
-        out_shape=jax.ShapeDtypeStruct(cycle.shape, f32),
-        in_specs=[anywhere] * len(args),
-        out_specs=anywhere,
-        input_output_aliases={} if base is None else {2: 0},
-        scratch_shapes=[
-            pltpu.VMEM((channels, held, cells // LANES, sector, LANES), f32),
-            pltpu.VMEM((channels, count, sector, cells), f32),
-            pltpu.VMEM((count, channels, tiles + SUB, cells), f32),
-            pltpu.VMEM((count, channels, tiles + SUB, cells), f32),
-            pltpu.SemaphoreType.DMA((chunks, cells // LANES)),
-            pltpu.SemaphoreType.DMA((chunks,)),
-        ],
+        out_shape=tuple(shapes),
+        in_specs=[whole, whole if handed_on else pl.BlockSpec(memory_space=pl.ANY)],
+        out_specs=(whole,) * len(shapes),
+        scratch_shapes=[pltpu.VMEM(edge, f32), pltpu.VMEM(edge, f32)],
         compiler_params=pltpu.CompilerParams(vmem_limit_bytes=GRANT),
         name="cycle_planes_%d" % first,
-    )(*args)
+    )(in_vmem(held), after)
 
 
 def pick(total, values, lanes, weights):
@@ -304,8 +258,9 @@
 SLOT = 32
 
 
-def outgoing_kernel(ring, cycle, core, taps, raw_weights, far_ref, near_ref, odd_ref, send_ref, keep_ref,
-                    core_ref, taps_ref, weights_ref, strip_ref, cycle_rows, side_ref, turn_ref, ends_ref, lane_ref, weight_ref, share_ref, sems):
+def outgoing_kernel(ring, cycle, core, taps, raw_weights, held_ref, far_ref, near_ref, odd_ref, send_ref,
+                    keep_ref, core_ref, taps_ref, weights_ref, side_ref, turn_ref, vals_ref, lane_ref,
+                    weight_ref, flag_ref, used_ref, share_ref, sems):
     channels, planes, sector, cells = cycle.shape
     core_rows, core_cells = core_ref.shape[2:]
     lead = channels * planes
@@ -316,22 +271,19 @@
     far = planes - 1 - near
     lane = lax.broadcasted_iota(jnp.int32, (1, LANES), 1)
     per = LANES // DEEP
-    strip = pltpu.make_async_copy(cycle.at[:, :, :, pl.ds(0, LANES)], strip_ref, sems.at[4])
+    early = [
+        pltpu.make_async_copy(core, core_ref, sems.at[0]),
+        pltpu.make_async_copy(taps, taps_ref, sems.at[1]),
+        pltpu.make_async_copy(raw_weights, weights_ref, sems.at[2]),
+    ]
+    cycle_strips = cells // LANES
     copies = [
-        pltpu.make_async_copy(cycle.at[:, :, pl.ds(0, SUB)], cycle_rows.at[0], sems.at[0]),
-        pltpu.make_async_copy(cycle.at[:, :, pl.ds(sector - SUB, SUB)], cycle_rows.at[1], sems.at[1]),
-        pltpu.make_async_copy(cycle.at[:, far], far_ref.at[:, pl.ds(0, sector)], sems.at[2]),
-        pltpu.make_async_copy(cycle.at[:, near], near_ref.at[:, pl.ds(0, sector)], sems.at[3]),
+        pltpu.make_async_copy(
+            cycle.at[:, :, :, pl.ds(n * LANES, LANES)], held_ref.at[:, :, n], sems.at[3 + n]
+        )
+        for n in range(cycle_strips)
     ]
-    early = [
-        pltpu.make_async_copy(core, core_ref, sems.at[5]),
-        pltpu.make_async_copy(taps, taps_ref, sems.at[6]),
-        pltpu.make_async_copy(raw_weights, weights_ref, sems.at[7]),
-    ]
-    for copy in early:
-        copy.start()
-    strip.start()
-    for copy in copies:
+    for copy in early + copies:
         copy.start()
     groups = ring // 2
     for copy in early:
@@ -363,71 +315,78 @@
             total = jnp.where(lane // SLOT == d, moved, total)
         sides.append(jnp.where(lane < DEEP * SLOT, total, 0.0))
 
+    whole = (strips - 1) * DEEP
+    slots = vals_ref.shape[0]
+    pairs = slots - 2 - whole
+    fold = DEEP // pairs
+    vals_ref[0] = sides[0]
+    vals_ref[1] = sides[1]
+    at_end = (own == 0) | (own == ring - 1)
+    base = jnp.where(own == 0, 0, core_rows - DEEP)
+
+    @pl.when(at_end)
+    def _():
+        if fold * width < LANES:
+            vals_ref[2:] = jnp.zeros((slots - 2, lead, LANES), f32)
+        for i in range(lead):
+            plane = core_ref[i // planes, i % planes]
+            rows = jnp.where(own == 0, plane[:DEEP], plane[core_rows - DEEP :])
+            for d in range(DEEP):
+                for s in range(strips - 1):
+                    vals_ref[2 + s * DEEP + d, i : i + 1, :] = rows[d : d + 1, s * LANES : (s + 1) * LANES]
+                at = (d % fold) * width
+                vals_ref[2 + whole + d // fold, i : i + 1, at : at + width] = rows[d : d + 1, (strips - 1) * LANES :]
+
     weights = norm_rows(weights_ref[...])
     cell = taps_ref[...]
     row = ((cell.astype(f32) + 0.5) * (1.0 / core_cells)).astype(jnp.int32)
     column = cell - row * core_cells
     row = row - own * core_rows
     here = (row >= 0) & (row < core_rows)
-    left = here & (column < DEEP)
-    right = here & (column >= core_cells - DEEP)
-    depth = jnp.where(column < DEEP, column, column - (core_cells - DEEP))
-    lane_ref[0] = jnp.where(left | right, depth * SLOT + row, 0)
-    weight_ref[0] = jnp.where(left, weights, 0.0)
-    weight_ref[1] = jnp.where(right, weights, 0.0)
+    left = column < DEEP
+    right = column >= core_cells - DEEP
+    side_lane = jnp.where(left, column, column - (core_cells - DEEP)) * SLOT + row
+    depth = row - base
+    tail = column >= (strips - 1) * LANES
+    end_slot = jnp.where(tail, whole + depth // fold, (column // LANES) * DEEP + depth) + 2
+    end_lane = jnp.where(tail, column - (strips - 1) * LANES + (depth % fold) * width, column % LANES)
+    inside = here & at_end & (depth >= 0) & (depth < DEEP)
+    slot = jnp.where(here & left, 0, jnp.where(here & right, 1, jnp.where(inside, end_slot, slots)))
+    lane_ref[...] = jnp.where(slot < 2, side_lane, jnp.where(slot < slots, end_lane, 0))
+    for d in range(slots):
+        mine = jnp.where(slot == d, weights, 0.0)
+        weight_ref[d] = mine
+        flag_ref[d : d + 1, :] = jnp.max(mine, axis=0, keepdims=True)
+    power = jnp.left_shift(1, lax.broadcasted_iota(jnp.int32, (slots, 1), 0)).astype(f32)
+    for s in range(ring):
+        most = jnp.max(flag_ref[:, s * sector : (s + 1) * sector], axis=1, keepdims=True)
+        used_ref[s] = jnp.sum(jnp.where(most > 0.0, power, 0.0)).astype(jnp.int32)
 
     @pl.loop(0, ring)
     def _(s):
         part = pl.ds(pl.multiple_of(s * sector, sector), sector)
-        lanes = lane_ref[0, :, part]
-        total = pick(None, sides[0], lanes, weight_ref[0, :, part])
-        share_ref[:, part] = pick(total, sides[1], lanes, weight_ref[1, :, part])
-
-    whole = (strips - 1) * DEEP
-    pairs = ends_ref.shape[0] - whole
-    fold = DEEP // pairs
-
-    @pl.when((own == 0) | (own == ring - 1))
-    def _():
-        base = jnp.where(own == 0, 0, core_rows - DEEP)
-        if fold * width < LANES:
-            ends_ref[...] = jnp.zeros_like(ends_ref)
-        for i in range(lead):
-            plane = core_ref[i // planes, i % planes]
-            rows = jnp.where(own == 0, plane[:DEEP], plane[core_rows - DEEP :])
-            for d in range(DEEP):
-                for s in range(strips - 1):
-                    ends_ref[s * DEEP + d, i : i + 1, :] = rows[d : d + 1, s * LANES : (s + 1) * LANES]
-                at = (d % fold) * width
-                ends_ref[whole + d // fold, i : i + 1, at : at + width] = rows[d : d + 1, (strips - 1) * LANES :]
-        inside = here & (column >= DEEP) & (column < core_cells - DEEP)
-        depth = row - base
-        inside = inside & (depth >= 0) & (depth < DEEP)
-        tail = column >= (strips - 1) * LANES
-        lane_ref[0] = jnp.where(
-            inside, jnp.where(tail, column - (strips - 1) * LANES + (depth % fold) * width, column % LANES), 0
-        )
-        for d in range(DEEP):
-            for s in range(strips - 1):
-                strip = inside & (column >= s * LANES) & (column < (s + 1) * LANES) & (depth == d)
-                weight_ref[s * DEEP + d] = jnp.where(strip, weights, 0.0)
-        for d in range(pairs):
-            strip = inside & tail & (depth >= d * fold) & (depth < (d + 1) * fold)
-            weight_ref[whole + d] = jnp.where(strip, weights, 0.0)
-
-        @pl.loop(0, ring)
-        def _(s):
-            part = pl.ds(pl.multiple_of(s * sector, sector), sector)
-            lanes = lane_ref[0, :, part]
-            total = share_ref[:, part]
-            for d in range(whole + pairs):
-                total = pick(total, ends_ref[d], lanes, weight_ref[d, :, part])
-            share_ref[:, part] = total
-
-    strip.wait()
+        share_ref[:, part] = jnp.zeros((lead, sector), f32)
+        used = used_ref[s]
+
+        def add(d):
+            @pl.when(lax.rem(lax.div(used, 1 << d), 2) == 1)
+            def _():
+                share_ref[:, part] = pick(
+                    share_ref[:, part], vals_ref[d], lane_ref[:, part], weight_ref[d, :, part]
+                )
+
+        add(0)
+        add(1)
+
+        @pl.when(used > 3)
+        def _():
+            for d in range(2, slots):
+                add(d)
+
+    copies[0].wait()
     trace = None
     for i in range(lead):
-        block = strip_ref[i // planes, i % planes]
+        block = held_ref[i // planes, i % planes, 0]
         moved = pltpu.roll(block, i, 1) if i else block
         trace = moved if trace is None else jnp.where(lane == i, moved, trace)
     trace = jnp.transpose(trace)[:lead]
@@ -449,16 +408,23 @@
     for c in range(channels):
         near_ref[c, sector:, 0:core_cells] = core_ref[c, near]
         far_ref[c, sector:, 0:core_cells] = core_ref[c, far]
-    for copy in copies:
+    for copy in copies[1:]:
         copy.wait()
+    for c in range(channels):
+        for n in range(cycle_strips):
+            wide = slice(n * LANES, (n + 1) * LANES)
+            near_ref[c, 0:sector, wide] = held_ref[c, near, n]
+            far_ref[c, 0:sector, wide] = held_ref[c, far, n]
     at = (groups + 1) * sector
     for c in range(channels):
         for x in range(planes):
             i = c * planes + x
-            low = cycle_rows[0, c, x, 0:1, :]
-            high = cycle_rows[1, c, x, SUB - 1 : SUB, :]
-            send_ref[i : i + 1, at : at + cells] = jnp.where(ring_even, high, low)
-            odd_ref[i : i + 1, 0:cells] = jnp.where(ring_even, low, high)
+            for n in range(cycle_strips):
+                low = held_ref[c, x, n, 0:1, :]
+                high = held_ref[c, x, n, sector - 1 : sector, :]
+                start = n * LANES
+                send_ref[i : i + 1, at + start : at + start + LANES] = jnp.where(ring_even, high, low)
+                odd_ref[i : i + 1, start : start + LANES] = jnp.where(ring_even, low, high)
             low = core_ref[c, x, 0:1, :]
             high = core_ref[c, x, core_rows - 1 : core_rows, :]
             send_ref[i : i + 1, at + cells : at + cells + core_cells] = jnp.where(ring_even, high, low)
@@ -472,7 +438,7 @@
     groups = ring // 2
     strips = -(-core_cells // LANES)
     fold = 2 if 2 * (core_cells - (strips - 1) * LANES) <= LANES else 1
-    slots = (strips - 1) * DEEP + DEEP // fold
+    slots = 2 + (strips - 1) * DEEP + DEEP // fold
     parts = -(-lead * DEEP // LANES)
     whole = pl.BlockSpec(memory_space=pltpu.VMEM)
     anywhere = pl.BlockSpec(memory_space=pl.ANY)
@@ -481,6 +447,7 @@
     return pl.pallas_call(
         functools.partial(outgoing_kernel, ring),
         out_shape=(
+            pltpu.VMEM((channels, planes, cells // LANES, sector, LANES), f32),
             plane,
             plane,
             jax.ShapeDtypeStruct((lead, edge), f32),
@@ -488,22 +455,23 @@
             jax.ShapeDtypeStruct((lead, groups * sector), f32),
         ),
         in_specs=[anywhere] * 4,
-        out_specs=(whole,) * 5,
+        out_specs=(whole,) * 6,
         scratch_shapes=[
             pltpu.VMEM(core.shape, f32),
             pltpu.VMEM(taps.shape, jnp.int32),
             pltpu.VMEM(weights.shape, f32),
-            pltpu.VMEM((channels, planes, sector, LANES), f32),
-            pltpu.VMEM((2, channels, planes, SUB, cells), f32),
             pltpu.VMEM((SLOT, LANES), f32),
             pltpu.VMEM((parts * LANES, LANES), f32),
             pltpu.VMEM((slots, lead, LANES), f32),
-            pltpu.VMEM((1,) + taps.shape, jnp.int32),
+            pltpu.VMEM(taps.shape, jnp.int32),
             pltpu.VMEM((slots,) + taps.shape, f32),
+            pltpu.VMEM((slots, taps.shape[1]), f32),
+            pltpu.SMEM((ring,), jnp.int32),
             pltpu.VMEM((lead, ring * sector), f32),
-            pltpu.SemaphoreType.DMA((8,)),
+            pltpu.SemaphoreType.DMA((3 + cells // LANES,)),
         ],
         compiler_params=pltpu.CompilerParams(vmem_limit_bytes=GRANT),
+        cost_estimate=pl.CostEstimate(flops=0, bytes_accessed=16 * 1024 * 1024, transcendentals=0),
         name="outgoing",
     )(in_hbm(cycle), in_hbm(core), in_hbm(taps), in_hbm(weights))
 
@@ -537,14 +505,14 @@
         out_specs=(whole,) * groups,
         compiler_params=pltpu.CompilerParams(vmem_limit_bytes=GRANT),
         name="ghost_relay",
-    )(sent, kept, got, in_hbm(after))
-
-
-def final_kernel(ring, core_ref, taps_ref, weights_ref, got_ref, odd_ref, near_ref, far_ref, partial, *rest):
+    )(sent, kept, got, after)
+
+
+def final_kernel(ring, core_ref, taps_ref, weights_ref, got_ref, odd_ref, near_ref, far_ref, lower, upper, *rest):
     groups = ring // 2
     blocks = rest[:groups]
-    (cycle_out, core_out, k_ref, next_ref, prev_ref, turn_ref, strip, wing, brim,
-     in_sem, out_sem) = rest[groups:]
+    (cycle_out, core_out, k_ref, next_ref, prev_ref, turn_ref, found_ref, strip, wing, brim,
+     out_sem) = rest[groups:]
     channels, planes, sector, cells = cycle_out.shape
     core_rows, core_cells = core_ref.shape[2:]
     lead = channels * planes
@@ -557,24 +525,26 @@
     middle = pl.ds(1, planes - 2)
     ends = (pl.ds(0, SUB), pl.ds(sector - SUB, SUB))
 
-    def places(ref):
-        found = [(ref.at[:, x, :, inner], strip.at[x]) for x in range(planes)]
-        found += [(ref.at[:, x, :, outer], wing.at[n]) for n, x in enumerate((0, planes - 1))]
-        found += [(ref.at[:, middle, ends[n], outer], brim.at[n]) for n in range(2)]
-        return found
-
-    def in_copies():
-        return [
-            pltpu.make_async_copy(a, b, in_sem.at[n]) for n, (a, b) in enumerate(places(partial))
-        ]
-
-    def out_copies():
-        return [
-            pltpu.make_async_copy(b, a, out_sem.at[n]) for n, (a, b) in enumerate(places(cycle_out))
-        ]
-
-    coming, leaving = in_copies(), out_copies()
-    for copy in coming:
+    half = lower.shape[1]
+
+    def block(x):
+        return (lower, x) if x < half else (upper, x - half)
+
+    bulk = pl.ds(SUB, sector - 2 * SUB)
+    places = [
+        (lower.at[:, pl.ds(1, half - 1), bulk, outer], cycle_out.at[:, pl.ds(1, half - 1), bulk, outer]),
+        (
+            upper.at[:, pl.ds(0, planes - 1 - half), bulk, outer],
+            cycle_out.at[:, pl.ds(half, planes - 1 - half), bulk, outer],
+        ),
+    ]
+    places += [(strip.at[x], cycle_out.at[:, x, :, inner]) for x in range(planes)]
+    places += [(wing.at[n], cycle_out.at[:, x, :, outer]) for n, x in enumerate((0, planes - 1))]
+    places += [(brim.at[n], cycle_out.at[:, middle, ends[n], outer]) for n in range(2)]
+    leaving = [
+        pltpu.make_async_copy(a, b, out_sem.at[n]) for n, (a, b) in enumerate(places)
+    ]
+    for copy in leaving[:2]:
         copy.start()
     lane = lax.broadcasted_iota(jnp.int32, (1, LANES), 1)
 
@@ -609,15 +579,24 @@
     taps, weights = targets(taps), targets(weights)
     lanes = taps % sector
     home = taps // sector
-    found = [None, None]
-    for s in range(groups):
-        for y in range(2):
-            values = blocks[s][:, (1 + y) * sector : (2 + y) * sector]
-            masked = jnp.where(home == 2 * (group ^ s) + y, weights, 0.0)
-            for h in range(2):
-                part = slice(h * LANES, (h + 1) * LANES)
-                found[h] = pick(found[h], values, lanes[:, part], masked[:, part])
-    found = jnp.concatenate(found, axis=1)
+    found_ref[1] = jnp.zeros((lead, LANES), f32)
+    def collect(h):
+        part = slice(h * LANES, (h + 1) * LANES)
+        total = None
+        for s in range(groups):
+            for y in range(2):
+                values = blocks[s][:, (1 + y) * sector : (2 + y) * sector]
+                masked = jnp.where(home[:, part] == 2 * (group ^ s) + y, weights[:, part], 0.0)
+                total = pick(total, values, lanes[:, part], masked)
+        found_ref[h] = total
+
+    collect(0)
+
+    @pl.when((own == 0) | (own == ring - 1))
+    def _():
+        collect(1)
+
+    found = jnp.concatenate([found_ref[0], found_ref[1]], axis=1)
     turn_ref[0:lead, :] = found[:, 0:LANES]
     sides = jnp.transpose(turn_ref[...])
     left_side = sides[0:core_rows]
@@ -625,13 +604,11 @@
     found = found[:, PAIR : PAIR + core_cells]
 
     for x in range(planes):
-        coming[x].wait()
+        part, at = block(x)
         for c in range(5):
             i = c * planes + x
             moved = pltpu.roll(gift, (LANES - i) % LANES, 1)
-            strip[x, c, :, :] += jnp.where(lane == 0, moved, 0.0)
-    for copy in coming[planes:]:
-        copy.wait()
+            strip[x, c] = part[c, at, :, 0:LANES] + jnp.where(lane == 0, moved, 0.0)
 
     def sides(q):
         u, pressure, enthalpy = velocities(q)
@@ -645,9 +622,10 @@
         _, low = sides([jnp.where(core_even, far[c], near[c]) for c in range(5)])
         high, _ = sides([jnp.where(core_even, near[c], far[c]) for c in range(5)])
         for n, value in enumerate((low, high)):
+            ref, at = block(n * (planes - 1))
             for c in range(5):
                 strip[n * (planes - 1), c, part, :] += value[c][:, :LANES]
-                wing[n, c, part, :] += value[c][:, LANES:]
+                wing[n, c, part, :] = ref[c, at, part, LANES:] + value[c][:, LANES:]
 
     _, radius_inv = radial_tables(cells)
     alpha2, beta2 = azim_coefs(radius_inv, 2.0 * math.pi / (sector * ring))
@@ -671,16 +649,19 @@
                 strip[x, c, at : at + 1, :] += value[c][x : x + 1, :LANES]
                 rest_row = value[c][x : x + 1, LANES:]
                 if 0 < x < planes - 1:
+                    ref, spot = block(x)
+                    brim[n, c, x - 1] = ref[c, spot, ends[n], LANES:]
                     brim[n, c, x - 1, small : small + 1, :] += rest_row
                 else:
                     wing[min(x, 1), c, at : at + 1, :] += rest_row
-    for copy in leaving:
+    for copy in leaving[2:]:
         copy.start()
 
     strips = k_ref.shape[2]
     padded = k_ref.shape[3]
     tail = strips * LANES - core_cells
     body = LANES - tail
+    both_sides = jnp.where(lane < lead, left_side, pltpu.roll(right_side, (body + 1) % LANES, 1))
     lows, highs = row_pair(cells, core_cells)
     for c in range(5):
         low, high = lows[c], highs[c]
@@ -692,11 +673,7 @@
             for s in range(strips - 1):
                 k_ref[c, x, s, 0:core_rows, :] = core_ref[c, x, :, s * LANES : (s + 1) * LANES]
             k_ref[c, x, strips - 1, 0:core_rows, 0:body] = core_ref[c, x, :, (strips - 1) * LANES :]
-            pad = jnp.where(
-                lane == LANES - 1,
-                pltpu.roll(left_side, (LANES - 1 - i) % LANES, 1),
-                pltpu.roll(right_side, (body - i) % LANES, 1),
-            )
+            pad = pltpu.roll(both_sides, (LANES - 1 - i) % LANES, 1)
             k_ref[c, x, strips - 1, 0:core_rows, body:] = pad[:, body:]
             for row, value in ((core_rows, high), (padded - 1, low)):
                 for s in range(strips - 1):
@@ -769,11 +746,12 @@
         copy.wait()
 
 
-def final_call(ring, core, taps, weights, got, odd, near, far, partial, blocks):
-    channels, planes, sector, cells = partial.shape
+def final_call(ring, shape, core, taps, weights, got, odd, near, far, lower, upper, blocks):
+    channels, planes, sector, cells = shape
     core_rows, core_cells = core.shape[2:]
     strips = -(-(core_cells + 2) // LANES)
     padded = -(-(core_rows + 2) // SUB) * SUB
+    lead = channels * planes
     whole = pl.BlockSpec(memory_space=pltpu.VMEM)
     anywhere = pl.BlockSpec(memory_space=pltpu.HBM)
     groups = ring // 2
@@ -781,26 +759,25 @@
     return pl.pallas_call(
         functools.partial(final_kernel, ring),
         out_shape=(
-            jax.ShapeDtypeStruct(partial.shape, f32),
+            jax.ShapeDtypeStruct(shape, f32),
             jax.ShapeDtypeStruct(core.shape, f32),
         ),
-        in_specs=[whole] * 7 + [anywhere] + [whole] * groups,
+        in_specs=[whole] * (9 + groups),
         out_specs=(anywhere, whole),
-        input_output_aliases={7: 0},
         scratch_shapes=[
             pltpu.VMEM((channels, planes, strips, padded, LANES), f32),
             pltpu.VMEM(edge_shape, f32),
             pltpu.VMEM(edge_shape, f32),
             pltpu.VMEM((LANES, LANES), f32),
+            pltpu.VMEM((2, lead, LANES), f32),
             pltpu.VMEM((planes, channels, sector, LANES), f32),
             pltpu.VMEM((2, channels, sector, cells - LANES), f32),
             pltpu.VMEM((2, channels, planes - 2, SUB, cells - LANES), f32),
-            pltpu.SemaphoreType.DMA((planes + 4,)),
-            pltpu.SemaphoreType.DMA((planes + 4,)),
+            pltpu.SemaphoreType.DMA((planes + 6,)),
         ],
         compiler_params=pltpu.CompilerParams(vmem_limit_bytes=GRANT),
         name="late_terms",
-    )(core, taps, weights, got, odd, near, far, partial, *blocks)
+    )(core, taps, weights, got, odd, near, far, in_vmem(lower), in_vmem(upper), *blocks)
 
 
 def body(cycle, core, core_taps, core_weights, cycle_taps, cycle_weights):
@@ -814,19 +791,21 @@
     even_azim = [(i, i ^ 1) for i in range(ring)]
     odd_azim = [(i, (i + 1) % ring) for i in range(1, ring, 2)]
     odd_azim += [(b, a) for a, b in odd_azim]
-    far, near, odd, sent, kept = outgoing_call(ring, cycle, core, cycle_taps.T, cycle_weights.T)
+    held, far, near, odd, sent, kept = outgoing_call(ring, cycle, core, cycle_taps.T, cycle_weights.T)
     got = lax.ppermute(sent, "azim", even_azim)
     far = lax.ppermute(far, "axial", odd_axial)
     near = lax.ppermute(near, "axial", even_axial)
+    half = planes // 2
+    lower, odd = main_call(0, half, angle_step, held, odd, True)
     odd = lax.ppermute(odd, "azim", odd_azim)
-    half = planes // 2
-    partial = main_call(0, half, angle_step, cycle, kept)
-    blocks = list(relay_call(ring, sector, sent, kept, got, partial))
-    partial = main_call(half, planes - half, angle_step, cycle, blocks[0], partial)
+    blocks = list(relay_call(ring, sector, sent, kept, got, lower))
+    (upper,) = main_call(half, planes - half, angle_step, held, blocks[0], False)
     for s in range(1, ring // 2):
         blocks[s] = lax.ppermute(blocks[s], "azim", [(i, i ^ (2 * s)) for i in range(ring)])
     return tuple(
-        final_call(ring, core, core_taps.T, core_weights.T, got, odd, near, far, partial, blocks)
+        final_call(
+            ring, cycle.shape, core, core_taps.T, core_weights.T, got, odd, near, far, lower, upper, blocks
+        )
     )
 
 

time: 37.6 us -> 32.7 us (0.87)
  Pallas kernels: 24.5 us -> 17.8 us
  starting transfers between devices: 12.1 us -> 13.5 us
  waiting for transfers between devices: 0.02 us -> 0.53 us
    pallas_call x2, Pallas kernels: 12.3 us -> 7.39 us  [main_call(): pl.pallas_call(functools.partial(main_kernel, first, count, angle_step),...]
    ppermute x3, starting transfers between devices: 4.45 us -> 5.7 us  [body(): lax.ppermute(blocks[s], 'azim', [(i, i ^ 2 * s) for i in range(ring)])]
    pallas_call x1, Pallas kernels: 6.45 us -> 5.43 us  [outgoing_call(): pl.pallas_call(functools.partial(outgoing_kernel, ring), out_shape=(pltpu...]
    pallas_call x1, Pallas kernels: 5.75 us -> 5 us  [final_call(): pl.pallas_call(functools.partial(final_kernel, ring), out_shape=(jax.Shap...]
    ppermute x1, waiting for transfers between devices: 0.01 us -> 0.51 us  [body(): odd = lax.ppermute(odd, 'azim', odd_azim)]
  transfers between devices with their start and end apart: 7 -> 7, of which waited for: 0 -> 1; matrix products, arithmetic and copies ran while one was open for 0% -> 0% of each run, Pallas kernels for 33% -> 23%
where the time goes in v2:
time: 32.7 us; the launch traced here: 32.6 us
  Pallas kernels  17.8 us (54%)
  starting transfers between devices  13.5 us (41%)
  between operations  0.73 us (2%)
  waiting for transfers between devices  0.53 us (2%)
    pallas_call x2, Pallas kernels, main_call(): pl.pallas_call(functools.partial(main_kernel, first, count, angle_step),...  7.39 us
    ppermute x3, starting transfers between devices, body(): lax.ppermute(blocks[s], 'azim', [(i, i ^ 2 * s) for i in range(ring)])  5.7 us
    pallas_call x1, Pallas kernels, outgoing_call(): pl.pallas_call(functools.partial(outgoing_kernel, ring), out_shape=(pltpu...  5.43 us
    pallas_call x1, Pallas kernels, final_call(): pl.pallas_call(functools.partial(final_kernel, ring), out_shape=(jax.Shap...  5 us
    ppermute x1, starting transfers between devices, body(): odd = lax.ppermute(odd, 'azim', odd_azim)  4.62 us
    ppermute x1, starting transfers between devices, body(): far = lax.ppermute(far, 'axial', odd_axial)  2.62 us
  transfers between devices with their start and end apart: 7, of which 1 were waited for; matrix products, arithmetic and copies ran while one was open for 0% of the time, Pallas kernels for 23%

profile of v2, /device:TPU:0, one launch (start us, length us, event | category | flops | bytes accessed | tf_op | source)
XLA Modules:
  0.0 32.6 jit_solution(4263395386615459290)
XLA Ops:
  0.6 5.4 %outgoing.1 = (f32[5,8,2,128,128]{4,3,2,1,0:T(8,128)S(1)}, f32[5,152,256]{2,1,0:T(8,128)S(1)}, f32[5,152,256]{2,1,0:T(8,128)S(1)}, f32[40,512]{1,0:T(8,128)S(1)}...) custom-call(f32[5,8,128,256]{3,2,1,0:T(8,128)} %cycle.1, f32[5,8,24,192]{3,2,1,0:T(8,128)} %core_ref.1, ...), custom_call_target="tpu_custom_call" | custom-call | bytes 16777216 | tf_op jit(solution)/shard_map/outgoing/pallas_call | solution.py:447
  6.1 0.5 %collective-permute-start.2 = (f32[5,152,256]{2,1,0:T(8,128)S(1)}, f32[5,152,256]{2,1,0:T(8,128)S(1)}, u32[]{:S(2)}, u32[]{:S(2)}) collective-permute-start(f32[5,152,256]{2,1,0:T(8,128)S(1)} %get-tuple-element.18), channel_id=1, source_target_pairs={{0,8},{8,0},{16,24},{24,16},{1,9},{9,1},{17,25},{25,17},{2,10},{10... | collective-permute-start | bytes 2334728 | tf_op jit(solution)/shard_map/ppermute | solution.py:797
  6.6 2.6 %collective-permute-start.3 = (f32[5,152,256]{2,1,0:T(8,128)S(1)}, f32[5,152,256]{2,1,0:T(8,128)S(1)}, u32[]{:S(2)}, u32[]{:S(2)}) collective-permute-start(f32[5,152,256]{2,1,0:T(8,128)S(1)} %get-tuple-element.19), channel_id=1, source_target_pairs={{8,16},{24,0},{16,8},{0,24},{9,17},{25,1},{17,9},{1,25},{10,18},{2... | collective-permute-start | bytes 2334728 | tf_op jit(solution)/shard_map/ppermute | solution.py:796
  9.2 0.0 collective-permute-start
  9.2 3.7 %cycle_planes_0.1 = (f32[5,4,128,256]{3,2,1,0:T(8,128)S(1)}, f32[40,512]{1,0:T(8,128)S(1)}) custom-call(f32[5,8,2,128,128]{4,3,2,1,0:T(8,128)S(1)} %get-tuple-element.15.q_ref, f32[40,512]{1,0:T(8,128)S(1)} %get-tuple-element.16.after), custom_call_target="tpu_custom_call" | custom-call | tf_op jit(solution)/shard_map/cycle_planes_0/pallas_call | solution.py:225
  12.9 4.6 %collective-permute-start.1 = (f32[40,512]{1,0:T(8,128)S(1)}, f32[40,512]{1,0:T(8,128)S(1)}, u32[]{:S(2)}, u32[]{:S(2)}) collective-permute-start(f32[40,512]{1,0:T(8,128)S(1)} %get-tuple-element.17), channel_id=1, source_target_pairs={{1,2},{3,4},{5,6},{7,0},{2,1},{4,3},{6,5},{0,7},{9,10},{11,12},{13... | collective-permute-start | bytes 245768 | tf_op jit(solution)/shard_map/ppermute | solution.py:800
  17.6 0.0 collective-permute-done.got.got_ref
  17.6 0.0 copy-start
  17.6 0.0 copy-start.1
  17.6 0.0 copy-start.2
  17.6 0.1 collective-permute-start.4
  17.7 2.2 %collective-permute-start.5 = (f32[40,384]{1,0:T(8,128)S(1)}, f32[40,384]{1,0:T(8,128)S(1)}, u32[]{:S(2)}, u32[]{:S(2)}) collective-permute-start(f32[40,384]{1,0:T(8,128)S(1)} %get-tuple-element.24), channel_id=1, source_target_pairs={{0,4},{1,5},{2,6},{3,7},{4,0},{5,1},{6,2},{7,3},{8,12},{9,13},{10,... | collective-permute-start | bytes 184328 | tf_op jit(solution)/shard_map/ppermute | solution.py:804
  19.9 0.5 %collective-permute-done.1.odd_ref = f32[40,512]{1,0:T(8,128)S(1)} collective-permute-done((f32[40,512]{1,0:T(8,128)S(1)}, f32[40,512]{1,0:T(8,128)S(1)}, u32[]{:S(2)}, u32[]{:S(2)}) %collective-permute-start.1) | collective-permute-done | bytes 81952 | tf_op jit(solution)/shard_map/ppermute | solution.py:800
  20.4 3.5 %collective-permute-start.6 = (f32[40,384]{1,0:T(8,128)S(1)}, f32[40,384]{1,0:T(8,128)S(1)}, u32[]{:S(2)}, u32[]{:S(2)}) collective-permute-start(f32[40,384]{1,0:T(8,128)S(1)} %get-tuple-element.25), channel_id=1, source_target_pairs={{0,6},{1,7},{2,4},{3,5},{4,2},{5,3},{6,0},{7,1},{8,14},{9,15},{10,... | collective-permute-start | bytes 184328 | tf_op jit(solution)/shard_map/ppermute | solution.py:804
  23.8 3.7 %cycle_planes_4.1.upper = f32[5,4,128,256]{3,2,1,0:T(8,128)S(1)} custom-call(f32[5,8,2,128,128]{4,3,2,1,0:T(8,128)S(1)} %get-tuple-element.15.q_ref, f32[40,384]{1,0:T(8,128)S(1)} %get-tuple-element.22.after.rest_0_), custom_call_target="tpu_custom_call" | custom-call | tf_op jit(solution)/shard_map/cycle_planes_4/pallas_call | solution.py:225
  27.5 0.0 collective-permute-done.4.rest_1_
  27.5 0.0 collective-permute-done.5.rest_2_
  27.5 0.0 collective-permute-done.6.rest_3_
  27.5 0.0 collective-permute-done.2.near_ref
  27.5 0.0 collective-permute-done.3.far_ref
  27.6 0.0 copy-done
  27.6 0.0 copy-done.1
  27.6 0.0 copy-done.2
  27.6 5.0 %late_terms.1 = (f32[5,8,128,256]{3,2,1,0:T(8,128)}, f32[5,8,24,192]{3,2,1,0:T(8,128)}) custom-call(f32[5,8,24,192]{3,2,1,0:T(8,128)S(1)} %copy-done, s32[4,768]{1,0:T(4,128)S(1)} %bitcast.4, f32[4,768]{1,0:T(4,128)S(1)} %bitcast.5, f32[40,1152]{1,0:T(8,128)S(1)} %collective-permute-done.got.got_ref, f32[40,512]{1,0:T(8,128)S(1)} %collective-permute-done.1.odd_ref, ...), custom_call_target="tpu_custom_call" | custom-call | tf_op jit(solution)/shard_map/late_terms/pallas_call | solution.py:759
  (1 shorter events, 0.0 us)
Async XLA Ops:
  6.1 21.5 %collective-permute-start.2 = (f32[5,152,256]{2,1,0:T(8,128)S(1)}, f32[5,152,256]{2,1,0:T(8,128)S(1)}, u32[]{:S(2)}, u32[]{:S(2)}) collective-permute-start(f32[5,152,256]{2,1,0:T(8,128)S(1)} %get-tuple-element.18), channel_id=1, source_target_pairs={{0,8},{8,0},{16,24},{24,16},{1,9},{9,1},{17,25},{25,17},{2,10},{10... | collective-permute-start | bytes 2334728 | tf_op jit(solution)/shard_map/ppermute | solution.py:797
  6.6 21.0 %collective-permute-start.3 = (f32[5,152,256]{2,1,0:T(8,128)S(1)}, f32[5,152,256]{2,1,0:T(8,128)S(1)}, u32[]{:S(2)}, u32[]{:S(2)}) collective-permute-start(f32[5,152,256]{2,1,0:T(8,128)S(1)} %get-tuple-element.19), channel_id=1, source_target_pairs={{8,16},{24,0},{16,8},{0,24},{9,17},{25,1},{17,9},{1,25},{10,18},{2... | collective-permute-start | bytes 2334728 | tf_op jit(solution)/shard_map/ppermute | solution.py:796
  9.2 8.4 %collective-permute-start = (f32[40,1152]{1,0:T(8,128)S(1)}, f32[40,1152]{1,0:T(8,128)S(1)}, u32[]{:S(2)}, u32[]{:S(2)}) collective-permute-start(f32[40,1152]{1,0:T(8,128)S(1)} %get-tuple-element.14.sent), channel_id=1, source_target_pairs={{0,1},{1,0},{2,3},{3,2},{4,5},{5,4},{6,7},{7,6},{8,9},{9,8},{10,11... | collective-permute-start | bytes 552968 | tf_op jit(solution)/shard_map/ppermute | solution.py:795
  12.9 7.4 %collective-permute-start.1 = (f32[40,512]{1,0:T(8,128)S(1)}, f32[40,512]{1,0:T(8,128)S(1)}, u32[]{:S(2)}, u32[]{:S(2)}) collective-permute-start(f32[40,512]{1,0:T(8,128)S(1)} %get-tuple-element.17), channel_id=1, source_target_pairs={{1,2},{3,4},{5,6},{7,0},{2,1},{4,3},{6,5},{0,7},{9,10},{11,12},{13... | collective-permute-start | bytes 245768 | tf_op jit(solution)/shard_map/ppermute | solution.py:800
  17.6 10.0 %copy-start = (f32[5,8,24,192]{3,2,1,0:T(8,128)S(1)}, f32[5,8,24,192]{3,2,1,0:T(8,128)}, u32[]{:S(2)}) copy-start(f32[5,8,24,192]{3,2,1,0:T(8,128)} %core_ref.1) | copy-start | bytes 2211844
  17.6 10.0 %copy-start.1 = (s32[768,4]{0,1:T(4,128)S(1)}, s32[768,4]{0,1:T(4,128)}, u32[]{:S(2)}) copy-start(s32[768,4]{0,1:T(4,128)} %param.8) | copy-start | bytes 36868
  17.6 10.0 %copy-start.2 = (f32[768,4]{0,1:T(4,128)S(1)}, f32[768,4]{0,1:T(4,128)}, u32[]{:S(2)}) copy-start(f32[768,4]{0,1:T(4,128)} %param.9) | copy-start | bytes 36868
  17.6 9.9 %collective-permute-start.4 = (f32[40,384]{1,0:T(8,128)S(1)}, f32[40,384]{1,0:T(8,128)S(1)}, u32[]{:S(2)}, u32[]{:S(2)}) collective-permute-start(f32[40,384]{1,0:T(8,128)S(1)} %get-tuple-element.23), channel_id=1, source_target_pairs={{0,2},{1,3},{2,0},{3,1},{4,6},{5,7},{6,4},{7,5},{8,10},{9,11},{10,... | collective-permute-start | bytes 184328 | tf_op jit(solution)/shard_map/ppermute | solution.py:804
  17.7 9.8 %collective-permute-start.5 = (f32[40,384]{1,0:T(8,128)S(1)}, f32[40,384]{1,0:T(8,128)S(1)}, u32[]{:S(2)}, u32[]{:S(2)}) collective-permute-start(f32[40,384]{1,0:T(8,128)S(1)} %get-tuple-element.24), channel_id=1, source_target_pairs={{0,4},{1,5},{2,6},{3,7},{4,0},{5,1},{6,2},{7,3},{8,12},{9,13},{10,... | collective-permute-start | bytes 184328 | tf_op jit(solution)/shard_map/ppermute | solution.py:804
  20.4 7.1 %collective-permute-start.6 = (f32[40,384]{1,0:T(8,128)S(1)}, f32[40,384]{1,0:T(8,128)S(1)}, u32[]{:S(2)}, u32[]{:S(2)}) collective-permute-start(f32[40,384]{1,0:T(8,128)S(1)} %get-tuple-element.25), channel_id=1, source_target_pairs={{0,6},{1,7},{2,4},{3,5},{4,2},{5,3},{6,0},{7,1},{8,14},{9,15},{10,... | collective-permute-start | bytes 184328 | tf_op jit(solution)/shard_map/ppermute | solution.py:804

commit v3 on v2

--- a/solution.py
+++ b/solution.py
@@ -258,7 +258,7 @@
 SLOT = 32
 
 
-def outgoing_kernel(ring, cycle, core, taps, raw_weights, held_ref, far_ref, near_ref, odd_ref, send_ref,
+def outgoing_kernel(ring, cycle, core, taps, raw_weights, held_ref, far_ref, near_ref, odd_ref, even_ref, send_ref,
                     keep_ref, core_ref, taps_ref, weights_ref, side_ref, turn_ref, vals_ref, lane_ref,
                     weight_ref, flag_ref, used_ref, share_ref, sems):
     channels, planes, sector, cells = cycle.shape
@@ -415,7 +415,6 @@
             wide = slice(n * LANES, (n + 1) * LANES)
             near_ref[c, 0:sector, wide] = held_ref[c, near, n]
             far_ref[c, 0:sector, wide] = held_ref[c, far, n]
-    at = (groups + 1) * sector
     for c in range(channels):
         for x in range(planes):
             i = c * planes + x
@@ -423,11 +422,11 @@
                 low = held_ref[c, x, n, 0:1, :]
                 high = held_ref[c, x, n, sector - 1 : sector, :]
                 start = n * LANES
-                send_ref[i : i + 1, at + start : at + start + LANES] = jnp.where(ring_even, high, low)
+                even_ref[i : i + 1, start : start + LANES] = jnp.where(ring_even, high, low)
                 odd_ref[i : i + 1, start : start + LANES] = jnp.where(ring_even, low, high)
             low = core_ref[c, x, 0:1, :]
             high = core_ref[c, x, core_rows - 1 : core_rows, :]
-            send_ref[i : i + 1, at + cells : at + cells + core_cells] = jnp.where(ring_even, high, low)
+            even_ref[i : i + 1, cells : cells + core_cells] = jnp.where(ring_even, high, low)
             odd_ref[i : i + 1, cells : cells + core_cells] = jnp.where(ring_even, low, high)
 
 
@@ -451,11 +450,12 @@
             plane,
             plane,
             jax.ShapeDtypeStruct((lead, edge), f32),
-            jax.ShapeDtypeStruct((lead, (groups + 1) * sector + edge), f32),
+            jax.ShapeDtypeStruct((lead, edge), f32),
+            jax.ShapeDtypeStruct((lead, (groups + 1) * sector), f32),
             jax.ShapeDtypeStruct((lead, groups * sector), f32),
         ),
         in_specs=[anywhere] * 4,
-        out_specs=(whole,) * 6,
+        out_specs=(whole,) * 7,
         scratch_shapes=[
             pltpu.VMEM(core.shape, f32),
             pltpu.VMEM(taps.shape, jnp.int32),
@@ -476,7 +476,8 @@
     )(in_hbm(cycle), in_hbm(core), in_hbm(taps), in_hbm(weights))
 
 
-def relay_kernel(groups, sent, kept, got, after, own_ref, *outs):
+def relay_kernel(groups, sent, kept, got, rows, after, rows_ref, own_ref, *outs):
+    rows_ref[...] = rows[...]
     sector = own_ref.shape[1] // 3
     own = lax.axis_index("azim")
     group = own // 2
@@ -494,21 +495,21 @@
         to[:, 2 * sector :] = second
 
 
-def relay_call(ring, sector, sent, kept, got, after):
+def relay_call(ring, sector, sent, kept, got, rows, after):
     groups = ring // 2
     whole = pl.BlockSpec(memory_space=pltpu.VMEM)
     block = jax.ShapeDtypeStruct((kept.shape[0], 3 * sector), f32)
     return pl.pallas_call(
         functools.partial(relay_kernel, groups),
-        out_shape=(block,) * groups,
-        in_specs=[whole] * 3 + [pl.BlockSpec(memory_space=pl.ANY)],
-        out_specs=(whole,) * groups,
+        out_shape=(jax.ShapeDtypeStruct(rows.shape, f32),) + (block,) * groups,
+        in_specs=[whole] * 4 + [pl.BlockSpec(memory_space=pl.ANY)],
+        out_specs=(whole,) * (1 + groups),
         compiler_params=pltpu.CompilerParams(vmem_limit_bytes=GRANT),
         name="ghost_relay",
-    )(sent, kept, got, after)
-
-
-def final_kernel(ring, core_ref, taps_ref, weights_ref, got_ref, odd_ref, near_ref, far_ref, lower, upper, *rest):
+    )(sent, kept, got, rows, after)
+
+
+def final_kernel(ring, core_ref, taps_ref, weights_ref, even_ref, odd_ref, near_ref, far_ref, lower, upper, *rest):
     groups = ring // 2
     blocks = rest[:groups]
     (cycle_out, core_out, k_ref, next_ref, prev_ref, turn_ref, found_ref, strip, wing, brim,
@@ -633,11 +634,10 @@
         pairs = []
         for c in range(5):
             odd = odd_ref[c * planes : (c + 1) * planes, start : start + width]
-            even = got_ref[c * planes : (c + 1) * planes, edge + start : edge + start + width]
+            even = even_ref[c * planes : (c + 1) * planes, start : start + width]
             pairs.append((jnp.where(ring_even, odd, even), jnp.where(ring_even, even, odd)))
         return [p[0] for p in pairs], [p[1] for p in pairs]
 
-    edge = (groups + 1) * sector
     low, high = row_pair(0, cells)
     _, low = edge_rows(low, alpha2, beta2)
     high, _ = edge_rows(high, alpha2, beta2)
@@ -746,7 +746,7 @@
         copy.wait()
 
 
-def final_call(ring, shape, core, taps, weights, got, odd, near, far, lower, upper, blocks):
+def final_call(ring, shape, core, taps, weights, even, odd, near, far, lower, upper, blocks):
     channels, planes, sector, cells = shape
     core_rows, core_cells = core.shape[2:]
     strips = -(-(core_cells + 2) // LANES)
@@ -777,7 +777,7 @@
         ],
         compiler_params=pltpu.CompilerParams(vmem_limit_bytes=GRANT),
         name="late_terms",
-    )(core, taps, weights, got, odd, near, far, in_vmem(lower), in_vmem(upper), *blocks)
+    )(core, taps, weights, even, odd, near, far, in_vmem(lower), in_vmem(upper), *blocks)
 
 
 def body(cycle, core, core_taps, core_weights, cycle_taps, cycle_weights):
@@ -791,20 +791,21 @@
     even_azim = [(i, i ^ 1) for i in range(ring)]
     odd_azim = [(i, (i + 1) % ring) for i in range(1, ring, 2)]
     odd_azim += [(b, a) for a, b in odd_azim]
-    held, far, near, odd, sent, kept = outgoing_call(ring, cycle, core, cycle_taps.T, cycle_weights.T)
+    held, far, near, odd, even, sent, kept = outgoing_call(ring, cycle, core, cycle_taps.T, cycle_weights.T)
     got = lax.ppermute(sent, "azim", even_azim)
     far = lax.ppermute(far, "axial", odd_axial)
     near = lax.ppermute(near, "axial", even_axial)
     half = planes // 2
-    lower, odd = main_call(0, half, angle_step, held, odd, True)
+    lower, even = main_call(0, half, angle_step, held, even, True)
+    even = lax.ppermute(even, "azim", even_azim)
+    odd, *blocks = relay_call(ring, sector, sent, kept, got, odd, lower)
     odd = lax.ppermute(odd, "azim", odd_azim)
-    blocks = list(relay_call(ring, sector, sent, kept, got, lower))
     (upper,) = main_call(half, planes - half, angle_step, held, blocks[0], False)
     for s in range(1, ring // 2):
         blocks[s] = lax.ppermute(blocks[s], "azim", [(i, i ^ (2 * s)) for i in range(ring)])
     return tuple(
         final_call(
-            ring, cycle.shape, core, core_taps.T, core_weights.T, got, odd, near, far, lower, upper, blocks
+            ring, cycle.shape, core, core_taps.T, core_weights.T, even, odd, near, far, lower, upper, blocks
         )
     )
 

time: 32.7 us -> 32.2 us (0.985)
  starting transfers between devices: 13.5 us -> 12.7 us
    ppermute x3, starting transfers between devices: 5.7 us -> 2.93 us  [body(): lax.ppermute(blocks[s], 'azim', [(i, i ^ 2 * s) for i in range(ring)])]
    ppermute x0 -> x1, starting transfers between devices: none -> 2.08 us  [body(): even = lax.ppermute(even, 'azim', even_azim)]
    ppermute x3, waiting for transfers between devices: 0.01 us -> 0.76 us  [body(): lax.ppermute(blocks[s], 'azim', [(i, i ^ 2 * s) for i in range(ring)])]
    ppermute x1, waiting for transfers between devices: 0.51 us -> 0.01 us  [body(): odd = lax.ppermute(odd, 'azim', odd_azim)]
  transfers between devices with their start and end apart: 7 -> 8, of which waited for: 1 -> 1; matrix products, arithmetic and copies ran while one was open for 0% -> 0% of each run, Pallas kernels for 23% -> 23%
where the time goes in v3:
time: 32.2 us; the launch traced here: 32.1 us
  Pallas kernels  17.8 us (55%)
  starting transfers between devices  12.7 us (39%)
  waiting for transfers between devices  0.78 us (2%)
  between operations  0.7 us (2%)
    pallas_call x2, Pallas kernels, main_call(): pl.pallas_call(functools.partial(main_kernel, first, count, angle_step),...  7.39 us
    pallas_call x1, Pallas kernels, outgoing_call(): pl.pallas_call(functools.partial(outgoing_kernel, ring), out_shape=(pltpu...  5.43 us
    pallas_call x1, Pallas kernels, final_call(): pl.pallas_call(functools.partial(final_kernel, ring), out_shape=(jax.Shap...  4.99 us
    ppermute x1, starting transfers between devices, body(): odd = lax.ppermute(odd, 'azim', odd_azim)  4.57 us
    ppermute x3, starting transfers between devices, body(): lax.ppermute(blocks[s], 'azim', [(i, i ^ 2 * s) for i in range(ring)])  2.93 us
    ppermute x1, starting transfers between devices, body(): far = lax.ppermute(far, 'axial', odd_axial)  2.62 us
    ppermute x1, starting transfers between devices, body(): even = lax.ppermute(even, 'azim', even_azim)  2.08 us
    ppermute x3, waiting for transfers between devices, body(): lax.ppermute(blocks[s], 'azim', [(i, i ^ 2 * s) for i in range(ring)])  0.76 us
  transfers between devices with their start and end apart: 8, of which 1 were waited for; matrix products, arithmetic and copies ran while one was open for 0% of the time, Pallas kernels for 23%

profile of v3, /device:TPU:0, one launch (start us, length us, event | category | flops | bytes accessed | tf_op | source)
XLA Modules:
  0.0 32.1 jit_solution(10847463076310604460)
XLA Ops:
  0.6 5.4 %outgoing.1 = (f32[5,8,2,128,128]{4,3,2,1,0:T(8,128)S(1)}, f32[5,152,256]{2,1,0:T(8,128)S(1)}, f32[5,152,256]{2,1,0:T(8,128)S(1)}, f32[40,512]{1,0:T(8,128)S(1)}...) custom-call(f32[5,8,128,256]{3,2,1,0:T(8,128)} %cycle.1, f32[5,8,24,192]{3,2,1,0:T(8,128)} %core_ref.1, ...), custom_call_target="tpu_custom_call" | custom-call | bytes 16777216 | tf_op jit(solution)/shard_map/outgoing/pallas_call | solution.py:446
  6.1 0.5 %collective-permute-start.3 = (f32[5,152,256]{2,1,0:T(8,128)S(1)}, f32[5,152,256]{2,1,0:T(8,128)S(1)}, u32[]{:S(2)}, u32[]{:S(2)}) collective-permute-start(f32[5,152,256]{2,1,0:T(8,128)S(1)} %get-tuple-element.24), channel_id=1, source_target_pairs={{0,8},{8,0},{16,24},{24,16},{1,9},{9,1},{17,25},{25,17},{2,10},{10... | collective-permute-start | bytes 2334728 | tf_op jit(solution)/shard_map/ppermute | solution.py:797
  6.6 2.6 %collective-permute-start.4 = (f32[5,152,256]{2,1,0:T(8,128)S(1)}, f32[5,152,256]{2,1,0:T(8,128)S(1)}, u32[]{:S(2)}, u32[]{:S(2)}) collective-permute-start(f32[5,152,256]{2,1,0:T(8,128)S(1)} %get-tuple-element.25), channel_id=1, source_target_pairs={{8,16},{24,0},{16,8},{0,24},{9,17},{25,1},{17,9},{1,25},{10,18},{2... | collective-permute-start | bytes 2334728 | tf_op jit(solution)/shard_map/ppermute | solution.py:796
  9.2 0.0 collective-permute-start.1
  9.2 3.7 %cycle_planes_0.1 = (f32[5,4,128,256]{3,2,1,0:T(8,128)S(1)}, f32[40,512]{1,0:T(8,128)S(1)}) custom-call(f32[5,8,2,128,128]{4,3,2,1,0:T(8,128)S(1)} %get-tuple-element.16.q_ref, f32[40,512]{1,0:T(8,128)S(1)} %get-tuple-element.17.after), custom_call_target="tpu_custom_call" | custom-call | tf_op jit(solution)/shard_map/cycle_planes_0/pallas_call | solution.py:225
  12.9 2.1 %collective-permute-start = (f32[40,512]{1,0:T(8,128)S(1)}, f32[40,512]{1,0:T(8,128)S(1)}, u32[]{:S(2)}, u32[]{:S(2)}) collective-permute-start(f32[40,512]{1,0:T(8,128)S(1)} %get-tuple-element.18), channel_id=1, source_target_pairs={{0,1},{1,0},{2,3},{3,2},{4,5},{5,4},{6,7},{7,6},{8,9},{9,8},{10,11... | collective-permute-start | bytes 245768 | tf_op jit(solution)/shard_map/ppermute | solution.py:800
  15.0 0.0 collective-permute-done.1.got
  15.0 0.0 copy-start
  15.0 0.0 copy-start.1
  15.0 0.0 copy-start.2
  15.1 0.1 collective-permute-start.5
  15.2 4.6 %collective-permute-start.2 = (f32[40,512]{1,0:T(8,128)S(1)}, f32[40,512]{1,0:T(8,128)S(1)}, u32[]{:S(2)}, u32[]{:S(2)}) collective-permute-start(f32[40,512]{1,0:T(8,128)S(1)} %get-tuple-element.23), channel_id=1, source_target_pairs={{1,2},{3,4},{5,6},{7,0},{2,1},{4,3},{6,5},{0,7},{9,10},{11,12},{13... | collective-permute-start | bytes 245768 | tf_op jit(solution)/shard_map/ppermute | solution.py:802
  19.8 0.0 collective-permute-done.even_ref
  19.8 0.3 collective-permute-start.6
  20.0 0.0 collective-permute-done.5.rest_1_
  20.0 2.5 %collective-permute-start.7 = (f32[40,384]{1,0:T(8,128)S(1)}, f32[40,384]{1,0:T(8,128)S(1)}, u32[]{:S(2)}, u32[]{:S(2)}) collective-permute-start(f32[40,384]{1,0:T(8,128)S(1)} %get-tuple-element.29), channel_id=1, source_target_pairs={{0,6},{1,7},{2,4},{3,5},{4,2},{5,3},{6,0},{7,1},{8,14},{9,15},{10,... | collective-permute-start | bytes 184328 | tf_op jit(solution)/shard_map/ppermute | solution.py:805
  22.6 3.7 %cycle_planes_4.1.upper = f32[5,4,128,256]{3,2,1,0:T(8,128)S(1)} custom-call(f32[5,8,2,128,128]{4,3,2,1,0:T(8,128)S(1)} %get-tuple-element.16.q_ref, f32[40,384]{1,0:T(8,128)S(1)} %get-tuple-element.26.after.rest_0_), custom_call_target="tpu_custom_call" | custom-call | tf_op jit(solution)/shard_map/cycle_planes_4/pallas_call | solution.py:225
  26.2 0.8 %collective-permute-done.6.rest_2_ = f32[40,384]{1,0:T(8,128)S(1)} collective-permute-done((f32[40,384]{1,0:T(8,128)S(1)}, f32[40,384]{1,0:T(8,128)S(1)}, u32[]{:S(2)}, u32[]{:S(2)}) %collective-permute-start.6) | collective-permute-done | bytes 61472 | tf_op jit(solution)/shard_map/ppermute | solution.py:805
  27.0 0.0 collective-permute-done.7.rest_3_
  27.0 0.0 collective-permute-done.2.odd_ref
  27.0 0.0 collective-permute-done.3.near_ref
  27.0 0.0 collective-permute-done.4.far_ref
  27.0 0.0 copy-done
  27.0 0.0 copy-done.1
  27.0 0.0 copy-done.2
  27.1 5.0 %late_terms.1 = (f32[5,8,128,256]{3,2,1,0:T(8,128)}, f32[5,8,24,192]{3,2,1,0:T(8,128)}) custom-call(f32[5,8,24,192]{3,2,1,0:T(8,128)S(1)} %copy-done, s32[4,768]{1,0:T(4,128)S(1)} %bitcast.4, f32[4,768]{1,0:T(4,128)S(1)} %bitcast.5, f32[40,512]{1,0:T(8,128)S(1)} %collective-permute-done.even_ref, f32[40,512]{1,0:T(8,128)S(1)} %collective-permute-done.2.odd_ref, ...), custom_call_target="tpu_custom_call" | custom-call | tf_op jit(solution)/shard_map/late_terms/pallas_call | solution.py:759
  (1 shorter events, 0.0 us)
Async XLA Ops:
  6.1 20.9 %collective-permute-start.3 = (f32[5,152,256]{2,1,0:T(8,128)S(1)}, f32[5,152,256]{2,1,0:T(8,128)S(1)}, u32[]{:S(2)}, u32[]{:S(2)}) collective-permute-start(f32[5,152,256]{2,1,0:T(8,128)S(1)} %get-tuple-element.24), channel_id=1, source_target_pairs={{0,8},{8,0},{16,24},{24,16},{1,9},{9,1},{17,25},{25,17},{2,10},{10... | collective-permute-start | bytes 2334728 | tf_op jit(solution)/shard_map/ppermute | solution.py:797
  6.6 20.4 %collective-permute-start.4 = (f32[5,152,256]{2,1,0:T(8,128)S(1)}, f32[5,152,256]{2,1,0:T(8,128)S(1)}, u32[]{:S(2)}, u32[]{:S(2)}) collective-permute-start(f32[5,152,256]{2,1,0:T(8,128)S(1)} %get-tuple-element.25), channel_id=1, source_target_pairs={{8,16},{24,0},{16,8},{0,24},{9,17},{25,1},{17,9},{1,25},{10,18},{2... | collective-permute-start | bytes 2334728 | tf_op jit(solution)/shard_map/ppermute | solution.py:796
  9.2 5.8 %collective-permute-start.1 = (f32[40,640]{1,0:T(8,128)S(1)}, f32[40,640]{1,0:T(8,128)S(1)}, u32[]{:S(2)}, u32[]{:S(2)}) collective-permute-start(f32[40,640]{1,0:T(8,128)S(1)} %get-tuple-element.19.sent), channel_id=1, source_target_pairs={{0,1},{1,0},{2,3},{3,2},{4,5},{5,4},{6,7},{7,6},{8,9},{9,8},{10,11... | collective-permute-start | bytes 307208 | tf_op jit(solution)/shard_map/ppermute | solution.py:795
  12.9 6.8 %collective-permute-start = (f32[40,512]{1,0:T(8,128)S(1)}, f32[40,512]{1,0:T(8,128)S(1)}, u32[]{:S(2)}, u32[]{:S(2)}) collective-permute-start(f32[40,512]{1,0:T(8,128)S(1)} %get-tuple-element.18), channel_id=1, source_target_pairs={{0,1},{1,0},{2,3},{3,2},{4,5},{5,4},{6,7},{7,6},{8,9},{9,8},{10,11... | collective-permute-start | bytes 245768 | tf_op jit(solution)/shard_map/ppermute | solution.py:800
  15.0 12.0 %copy-start = (f32[5,8,24,192]{3,2,1,0:T(8,128)S(1)}, f32[5,8,24,192]{3,2,1,0:T(8,128)}, u32[]{:S(2)}) copy-start(f32[5,8,24,192]{3,2,1,0:T(8,128)} %core_ref.1) | copy-start | bytes 2211844
  15.0 12.0 %copy-start.1 = (s32[768,4]{0,1:T(4,128)S(1)}, s32[768,4]{0,1:T(4,128)}, u32[]{:S(2)}) copy-start(s32[768,4]{0,1:T(4,128)} %param.8) | copy-start | bytes 36868
  15.0 12.0 %copy-start.2 = (f32[768,4]{0,1:T(4,128)S(1)}, f32[768,4]{0,1:T(4,128)}, u32[]{:S(2)}) copy-start(f32[768,4]{0,1:T(4,128)} %param.9) | copy-start | bytes 36868
  15.1 5.0 %collective-permute-start.5 = (f32[40,384]{1,0:T(8,128)S(1)}, f32[40,384]{1,0:T(8,128)S(1)}, u32[]{:S(2)}, u32[]{:S(2)}) collective-permute-start(f32[40,384]{1,0:T(8,128)S(1)} %get-tuple-element.27), channel_id=1, source_target_pairs={{0,2},{1,3},{2,0},{3,1},{4,6},{5,7},{6,4},{7,5},{8,10},{9,11},{10,... | collective-permute-start | bytes 184328 | tf_op jit(solution)/shard_map/ppermute | solution.py:805
  15.2 11.8 %collective-permute-start.2 = (f32[40,512]{1,0:T(8,128)S(1)}, f32[40,512]{1,0:T(8,128)S(1)}, u32[]{:S(2)}, u32[]{:S(2)}) collective-permute-start(f32[40,512]{1,0:T(8,128)S(1)} %get-tuple-element.23), channel_id=1, source_target_pairs={{1,2},{3,4},{5,6},{7,0},{2,1},{4,3},{6,5},{0,7},{9,10},{11,12},{13... | collective-permute-start | bytes 245768 | tf_op jit(solution)/shard_map/ppermute | solution.py:802
  19.8 7.2 %collective-permute-start.6 = (f32[40,384]{1,0:T(8,128)S(1)}, f32[40,384]{1,0:T(8,128)S(1)}, u32[]{:S(2)}, u32[]{:S(2)}) collective-permute-start(f32[40,384]{1,0:T(8,128)S(1)} %get-tuple-element.28), channel_id=1, source_target_pairs={{0,4},{1,5},{2,6},{3,7},{4,0},{5,1},{6,2},{7,3},{8,12},{9,13},{10,... | collective-permute-start | bytes 184328 | tf_op jit(solution)/shard_map/ppermute | solution.py:805
  20.0 7.0 %collective-permute-start.7 = (f32[40,384]{1,0:T(8,128)S(1)}, f32[40,384]{1,0:T(8,128)S(1)}, u32[]{:S(2)}, u32[]{:S(2)}) collective-permute-start(f32[40,384]{1,0:T(8,128)S(1)} %get-tuple-element.29), channel_id=1, source_target_pairs={{0,6},{1,7},{2,4},{3,5},{4,2},{5,3},{6,0},{7,1},{8,14},{9,15},{10,... | collective-permute-start | bytes 184328 | tf_op jit(solution)/shard_map/ppermute | solution.py:805

commit v4 on v3

--- a/solution.py
+++ b/solution.py
@@ -793,9 +793,9 @@
     odd_azim += [(b, a) for a, b in odd_azim]
     held, far, near, odd, even, sent, kept = outgoing_call(ring, cycle, core, cycle_taps.T, cycle_weights.T)
     got = lax.ppermute(sent, "azim", even_azim)
+    near = lax.ppermute(near, "axial", even_axial)
     far = lax.ppermute(far, "axial", odd_axial)
-    near = lax.ppermute(near, "axial", even_axial)
-    half = planes // 2
+    half = planes // 2 - 1
     lower, even = main_call(0, half, angle_step, held, even, True)
     even = lax.ppermute(even, "azim", even_azim)
     odd, *blocks = relay_call(ring, sector, sent, kept, got, odd, lower)

time: 32.2 us -> 32 us (level)
    ppermute x3, waiting for transfers between devices: 0.76 us -> 0.01 us  [body(): lax.ppermute(blocks[s], 'azim', [(i, i ^ 2 * s) for i in range(ring)])]
    ppermute x1, waiting for transfers between devices: 0.01 us -> 0.49 us  [body(): far = lax.ppermute(far, 'axial', odd_axial)]
where the time goes in v4:
time: 32 us; the launch traced here: 31.9 us
  Pallas kernels  17.8 us (56%)
  starting transfers between devices  12.8 us (40%)
  between operations  0.7 us (2%)
  waiting for transfers between devices  0.51 us (2%)
    pallas_call x2, Pallas kernels, main_call(): pl.pallas_call(functools.partial(main_kernel, first, count, angle_step),...  7.37 us
    pallas_call x1, Pallas kernels, outgoing_call(): pl.pallas_call(functools.partial(outgoing_kernel, ring), out_shape=(pltpu...  5.44 us
    pallas_call x1, Pallas kernels, final_call(): pl.pallas_call(functools.partial(final_kernel, ring), out_shape=(jax.Shap...  5 us
    ppermute x1, starting transfers between devices, body(): odd = lax.ppermute(odd, 'azim', odd_azim)  4.57 us
    ppermute x3, starting transfers between devices, body(): lax.ppermute(blocks[s], 'azim', [(i, i ^ 2 * s) for i in range(ring)])  3.01 us
    ppermute x1, starting transfers between devices, body(): far = lax.ppermute(far, 'axial', odd_axial)  2.62 us
    ppermute x1, starting transfers between devices, body(): even = lax.ppermute(even, 'azim', even_azim)  2.08 us
  transfers between devices with their start and end apart: 8, of which 1 were waited for; matrix products, arithmetic and copies ran while one was open for 0% of the time, Pallas kernels for 23%

profile of v4, /device:TPU:0, one launch (start us, length us, event | category | flops | bytes accessed | tf_op | source)
XLA Modules:
  0.0 31.9 jit_solution(1282010237185579248)
XLA Ops:
  0.6 5.4 %outgoing.1 = (f32[5,8,2,128,128]{4,3,2,1,0:T(8,128)S(1)}, f32[5,152,256]{2,1,0:T(8,128)S(1)}, f32[5,152,256]{2,1,0:T(8,128)S(1)}, f32[40,512]{1,0:T(8,128)S(1)}...) custom-call(f32[5,8,128,256]{3,2,1,0:T(8,128)} %cycle.1, f32[5,8,24,192]{3,2,1,0:T(8,128)} %core_ref.1, ...), custom_call_target="tpu_custom_call" | custom-call | bytes 16777216 | tf_op jit(solution)/shard_map/outgoing/pallas_call | solution.py:446
  6.1 0.5 %collective-permute-start.3 = (f32[5,152,256]{2,1,0:T(8,128)S(1)}, f32[5,152,256]{2,1,0:T(8,128)S(1)}, u32[]{:S(2)}, u32[]{:S(2)}) collective-permute-start(f32[5,152,256]{2,1,0:T(8,128)S(1)} %get-tuple-element.24), channel_id=1, source_target_pairs={{0,8},{8,0},{16,24},{24,16},{1,9},{9,1},{17,25},{25,17},{2,10},{10... | collective-permute-start | bytes 2334728 | tf_op jit(solution)/shard_map/ppermute | solution.py:796
  6.6 2.6 %collective-permute-start.4 = (f32[5,152,256]{2,1,0:T(8,128)S(1)}, f32[5,152,256]{2,1,0:T(8,128)S(1)}, u32[]{:S(2)}, u32[]{:S(2)}) collective-permute-start(f32[5,152,256]{2,1,0:T(8,128)S(1)} %get-tuple-element.25), channel_id=1, source_target_pairs={{8,16},{24,0},{16,8},{0,24},{9,17},{25,1},{17,9},{1,25},{10,18},{2... | collective-permute-start | bytes 2334728 | tf_op jit(solution)/shard_map/ppermute | solution.py:797
  9.2 0.0 collective-permute-start.1
  9.2 2.8 %cycle_planes_0.1 = (f32[5,3,128,256]{3,2,1,0:T(8,128)S(1)}, f32[40,512]{1,0:T(8,128)S(1)}) custom-call(f32[5,8,2,128,128]{4,3,2,1,0:T(8,128)S(1)} %get-tuple-element.16.q_ref, f32[40,512]{1,0:T(8,128)S(1)} %get-tuple-element.17.after), custom_call_target="tpu_custom_call" | custom-call | tf_op jit(solution)/shard_map/cycle_planes_0/pallas_call | solution.py:225
  12.1 2.1 %collective-permute-start = (f32[40,512]{1,0:T(8,128)S(1)}, f32[40,512]{1,0:T(8,128)S(1)}, u32[]{:S(2)}, u32[]{:S(2)}) collective-permute-start(f32[40,512]{1,0:T(8,128)S(1)} %get-tuple-element.18), channel_id=1, source_target_pairs={{0,1},{1,0},{2,3},{3,2},{4,5},{5,4},{6,7},{7,6},{8,9},{9,8},{10,11... | collective-permute-start | bytes 245768 | tf_op jit(solution)/shard_map/ppermute | solution.py:800
  14.1 0.0 collective-permute-done.1.got
  14.1 0.0 copy-start
  14.1 0.0 copy-start.1
  14.1 0.0 copy-start.2
  14.2 0.1 collective-permute-start.5
  14.3 4.6 %collective-permute-start.2 = (f32[40,512]{1,0:T(8,128)S(1)}, f32[40,512]{1,0:T(8,128)S(1)}, u32[]{:S(2)}, u32[]{:S(2)}) collective-permute-start(f32[40,512]{1,0:T(8,128)S(1)} %get-tuple-element.23), channel_id=1, source_target_pairs={{1,2},{3,4},{5,6},{7,0},{2,1},{4,3},{6,5},{0,7},{9,10},{11,12},{13... | collective-permute-start | bytes 245768 | tf_op jit(solution)/shard_map/ppermute | solution.py:802
  18.9 0.0 collective-permute-done.even_ref
  18.9 0.3 collective-permute-start.6
  19.2 0.0 collective-permute-done.5.rest_1_
  19.2 2.6 %collective-permute-start.7 = (f32[40,384]{1,0:T(8,128)S(1)}, f32[40,384]{1,0:T(8,128)S(1)}, u32[]{:S(2)}, u32[]{:S(2)}) collective-permute-start(f32[40,384]{1,0:T(8,128)S(1)} %get-tuple-element.29), channel_id=1, source_target_pairs={{0,6},{1,7},{2,4},{3,5},{4,2},{5,3},{6,0},{7,1},{8,14},{9,15},{10,... | collective-permute-start | bytes 184328 | tf_op jit(solution)/shard_map/ppermute | solution.py:805
  21.8 4.5 %cycle_planes_3.1.upper = f32[5,5,128,256]{3,2,1,0:T(8,128)S(1)} custom-call(f32[5,8,2,128,128]{4,3,2,1,0:T(8,128)S(1)} %get-tuple-element.16.q_ref, f32[40,384]{1,0:T(8,128)S(1)} %get-tuple-element.26.after.rest_0_), custom_call_target="tpu_custom_call" | custom-call | tf_op jit(solution)/shard_map/cycle_planes_3/pallas_call | solution.py:225
  26.3 0.0 collective-permute-done.6.rest_2_
  26.3 0.0 collective-permute-done.7.rest_3_
  26.3 0.0 collective-permute-done.2.odd_ref
  26.4 0.0 collective-permute-done.3.near_ref
  26.4 0.5 %collective-permute-done.4.far_ref = f32[5,152,256]{2,1,0:T(8,128)S(1)} collective-permute-done((f32[5,152,256]{2,1,0:T(8,128)S(1)}, f32[5,152,256]{2,1,0:T(8,128)S(1)}, u32[]{:S(2)}, u32[]{:S(2)}) %collective-permute-start.4) | collective-permute-done | bytes 778272 | tf_op jit(solution)/shard_map/ppermute | solution.py:797
  26.9 0.0 copy-done
  26.9 0.0 copy-done.1
  26.9 0.0 copy-done.2
  26.9 5.0 %late_terms.1 = (f32[5,8,128,256]{3,2,1,0:T(8,128)}, f32[5,8,24,192]{3,2,1,0:T(8,128)}) custom-call(f32[5,8,24,192]{3,2,1,0:T(8,128)S(1)} %copy-done, s32[4,768]{1,0:T(4,128)S(1)} %bitcast.4, f32[4,768]{1,0:T(4,128)S(1)} %bitcast.5, f32[40,512]{1,0:T(8,128)S(1)} %collective-permute-done.even_ref, f32[40,512]{1,0:T(8,128)S(1)} %collective-permute-done.2.odd_ref, ...), custom_call_target="tpu_custom_call" | custom-call | tf_op jit(solution)/shard_map/late_terms/pallas_call | solution.py:759
  (1 shorter events, 0.0 us)
Async XLA Ops:
  6.1 20.3 %collective-permute-start.3 = (f32[5,152,256]{2,1,0:T(8,128)S(1)}, f32[5,152,256]{2,1,0:T(8,128)S(1)}, u32[]{:S(2)}, u32[]{:S(2)}) collective-permute-start(f32[5,152,256]{2,1,0:T(8,128)S(1)} %get-tuple-element.24), channel_id=1, source_target_pairs={{0,8},{8,0},{16,24},{24,16},{1,9},{9,1},{17,25},{25,17},{2,10},{10... | collective-permute-start | bytes 2334728 | tf_op jit(solution)/shard_map/ppermute | solution.py:796
  6.6 20.3 %collective-permute-start.4 = (f32[5,152,256]{2,1,0:T(8,128)S(1)}, f32[5,152,256]{2,1,0:T(8,128)S(1)}, u32[]{:S(2)}, u32[]{:S(2)}) collective-permute-start(f32[5,152,256]{2,1,0:T(8,128)S(1)} %get-tuple-element.25), channel_id=1, source_target_pairs={{8,16},{24,0},{16,8},{0,24},{9,17},{25,1},{17,9},{1,25},{10,18},{2... | collective-permute-start | bytes 2334728 | tf_op jit(solution)/shard_map/ppermute | solution.py:797
  9.2 4.9 %collective-permute-start.1 = (f32[40,640]{1,0:T(8,128)S(1)}, f32[40,640]{1,0:T(8,128)S(1)}, u32[]{:S(2)}, u32[]{:S(2)}) collective-permute-start(f32[40,640]{1,0:T(8,128)S(1)} %get-tuple-element.19.sent), channel_id=1, source_target_pairs={{0,1},{1,0},{2,3},{3,2},{4,5},{5,4},{6,7},{7,6},{8,9},{9,8},{10,11... | collective-permute-start | bytes 307208 | tf_op jit(solution)/shard_map/ppermute | solution.py:795
  12.1 6.8 %collective-permute-start = (f32[40,512]{1,0:T(8,128)S(1)}, f32[40,512]{1,0:T(8,128)S(1)}, u32[]{:S(2)}, u32[]{:S(2)}) collective-permute-start(f32[40,512]{1,0:T(8,128)S(1)} %get-tuple-element.18), channel_id=1, source_target_pairs={{0,1},{1,0},{2,3},{3,2},{4,5},{5,4},{6,7},{7,6},{8,9},{9,8},{10,11... | collective-permute-start | bytes 245768 | tf_op jit(solution)/shard_map/ppermute | solution.py:800
  14.1 12.7 %copy-start = (f32[5,8,24,192]{3,2,1,0:T(8,128)S(1)}, f32[5,8,24,192]{3,2,1,0:T(8,128)}, u32[]{:S(2)}) copy-start(f32[5,8,24,192]{3,2,1,0:T(8,128)} %core_ref.1) | copy-start | bytes 2211844
  14.1 12.7 %copy-start.1 = (s32[768,4]{0,1:T(4,128)S(1)}, s32[768,4]{0,1:T(4,128)}, u32[]{:S(2)}) copy-start(s32[768,4]{0,1:T(4,128)} %param.8) | copy-start | bytes 36868
  14.1 12.7 %copy-start.2 = (f32[768,4]{0,1:T(4,128)S(1)}, f32[768,4]{0,1:T(4,128)}, u32[]{:S(2)}) copy-start(f32[768,4]{0,1:T(4,128)} %param.9) | copy-start | bytes 36868
  14.2 5.0 %collective-permute-start.5 = (f32[40,384]{1,0:T(8,128)S(1)}, f32[40,384]{1,0:T(8,128)S(1)}, u32[]{:S(2)}, u32[]{:S(2)}) collective-permute-start(f32[40,384]{1,0:T(8,128)S(1)} %get-tuple-element.27), channel_id=1, source_target_pairs={{0,2},{1,3},{2,0},{3,1},{4,6},{5,7},{6,4},{7,5},{8,10},{9,11},{10,... | collective-permute-start | bytes 184328 | tf_op jit(solution)/shard_map/ppermute | solution.py:805
  14.3 12.0 %collective-permute-start.2 = (f32[40,512]{1,0:T(8,128)S(1)}, f32[40,512]{1,0:T(8,128)S(1)}, u32[]{:S(2)}, u32[]{:S(2)}) collective-permute-start(f32[40,512]{1,0:T(8,128)S(1)} %get-tuple-element.23), channel_id=1, source_target_pairs={{1,2},{3,4},{5,6},{7,0},{2,1},{4,3},{6,5},{0,7},{9,10},{11,12},{13... | collective-permute-start | bytes 245768 | tf_op jit(solution)/shard_map/ppermute | solution.py:802
  18.9 7.4 %collective-permute-start.6 = (f32[40,384]{1,0:T(8,128)S(1)}, f32[40,384]{1,0:T(8,128)S(1)}, u32[]{:S(2)}, u32[]{:S(2)}) collective-permute-start(f32[40,384]{1,0:T(8,128)S(1)} %get-tuple-element.28), channel_id=1, source_target_pairs={{0,4},{1,5},{2,6},{3,7},{4,0},{5,1},{6,2},{7,3},{8,12},{9,13},{10,... | collective-permute-start | bytes 184328 | tf_op jit(solution)/shard_map/ppermute | solution.py:805
  19.2 7.2 %collective-permute-start.7 = (f32[40,384]{1,0:T(8,128)S(1)}, f32[40,384]{1,0:T(8,128)S(1)}, u32[]{:S(2)}, u32[]{:S(2)}) collective-permute-start(f32[40,384]{1,0:T(8,128)S(1)} %get-tuple-element.29), channel_id=1, source_target_pairs={{0,6},{1,7},{2,4},{3,5},{4,2},{5,3},{6,0},{7,1},{8,14},{9,15},{10,... | collective-permute-start | bytes 184328 | tf_op jit(solution)/shard_map/ppermute | solution.py:805

commit v5 on v4

--- a/solution.py
+++ b/solution.py
@@ -209,7 +209,7 @@
             before = [axial(q, -1.0) for q in load(first + count)]
         finish(count - 1, held, before)
 
-    @pl.loop(0, tiles)
+    @pl.loop(0, tiles, unroll=2)
     def _(j):
         tile(j)
 

time: 32 us -> 32 us (level)
  no operation moved by 1% of the time
where the time goes in v5:
time: 32 us; the launch traced here: 31.9 us
  Pallas kernels  17.7 us (55%)
  starting transfers between devices  12.9 us (40%)
  between operations  0.7 us (2%)
  waiting for transfers between devices  0.62 us (2%)
    pallas_call x2, Pallas kernels, main_call(): pl.pallas_call(functools.partial(main_kernel, first, count, angle_step),...  7.19 us
    pallas_call x1, Pallas kernels, outgoing_call(): pl.pallas_call(functools.partial(outgoing_kernel, ring), out_shape=(pltpu...  5.44 us
    pallas_call x1, Pallas kernels, final_call(): pl.pallas_call(functools.partial(final_kernel, ring), out_shape=(jax.Shap...  5 us
    ppermute x1, starting transfers between devices, body(): odd = lax.ppermute(odd, 'azim', odd_azim)  4.57 us
    ppermute x3, starting transfers between devices, body(): lax.ppermute(blocks[s], 'azim', [(i, i ^ 2 * s) for i in range(ring)])  3.08 us
    ppermute x1, starting transfers between devices, body(): far = lax.ppermute(far, 'axial', odd_axial)  2.62 us
    ppermute x1, starting transfers between devices, body(): even = lax.ppermute(even, 'azim', even_azim)  2.08 us
  transfers between devices with their start and end apart: 8, of which 1 were waited for; matrix products, arithmetic and copies ran while one was open for 0% of the time, Pallas kernels for 23%

profile of v5, /device:TPU:0, one launch (start us, length us, event | category | flops | bytes accessed | tf_op | source)
XLA Modules:
  0.0 31.9 jit_solution(11151785351207987806)
XLA Ops:
  0.6 5.4 %outgoing.1 = (f32[5,8,2,128,128]{4,3,2,1,0:T(8,128)S(1)}, f32[5,152,256]{2,1,0:T(8,128)S(1)}, f32[5,152,256]{2,1,0:T(8,128)S(1)}, f32[40,512]{1,0:T(8,128)S(1)}...) custom-call(f32[5,8,128,256]{3,2,1,0:T(8,128)} %cycle.1, f32[5,8,24,192]{3,2,1,0:T(8,128)} %core_ref.1, ...), custom_call_target="tpu_custom_call" | custom-call | bytes 16777216 | tf_op jit(solution)/shard_map/outgoing/pallas_call | solution.py:446
  6.1 0.5 %collective-permute-start.3 = (f32[5,152,256]{2,1,0:T(8,128)S(1)}, f32[5,152,256]{2,1,0:T(8,128)S(1)}, u32[]{:S(2)}, u32[]{:S(2)}) collective-permute-start(f32[5,152,256]{2,1,0:T(8,128)S(1)} %get-tuple-element.24), channel_id=1, source_target_pairs={{0,8},{8,0},{16,24},{24,16},{1,9},{9,1},{17,25},{25,17},{2,10},{10... | collective-permute-start | bytes 2334728 | tf_op jit(solution)/shard_map/ppermute | solution.py:796
  6.6 2.6 %collective-permute-start.4 = (f32[5,152,256]{2,1,0:T(8,128)S(1)}, f32[5,152,256]{2,1,0:T(8,128)S(1)}, u32[]{:S(2)}, u32[]{:S(2)}) collective-permute-start(f32[5,152,256]{2,1,0:T(8,128)S(1)} %get-tuple-element.25), channel_id=1, source_target_pairs={{8,16},{24,0},{16,8},{0,24},{9,17},{25,1},{17,9},{1,25},{10,18},{2... | collective-permute-start | bytes 2334728 | tf_op jit(solution)/shard_map/ppermute | solution.py:797
  9.2 0.0 collective-permute-start.1
  9.2 2.8 %cycle_planes_0.1 = (f32[5,3,128,256]{3,2,1,0:T(8,128)S(1)}, f32[40,512]{1,0:T(8,128)S(1)}) custom-call(f32[5,8,2,128,128]{4,3,2,1,0:T(8,128)S(1)} %get-tuple-element.16.q_ref, f32[40,512]{1,0:T(8,128)S(1)} %get-tuple-element.17.after), custom_call_target="tpu_custom_call" | custom-call | tf_op jit(solution)/shard_map/cycle_planes_0/pallas_call | solution.py:225
  12.0 2.1 %collective-permute-start = (f32[40,512]{1,0:T(8,128)S(1)}, f32[40,512]{1,0:T(8,128)S(1)}, u32[]{:S(2)}, u32[]{:S(2)}) collective-permute-start(f32[40,512]{1,0:T(8,128)S(1)} %get-tuple-element.18), channel_id=1, source_target_pairs={{0,1},{1,0},{2,3},{3,2},{4,5},{5,4},{6,7},{7,6},{8,9},{9,8},{10,11... | collective-permute-start | bytes 245768 | tf_op jit(solution)/shard_map/ppermute | solution.py:800
  14.1 0.0 collective-permute-done.1.got
  14.1 0.0 copy-start
  14.1 0.0 copy-start.1
  14.1 0.0 copy-start.2
  14.1 0.1 collective-permute-start.5
  14.3 4.6 %collective-permute-start.2 = (f32[40,512]{1,0:T(8,128)S(1)}, f32[40,512]{1,0:T(8,128)S(1)}, u32[]{:S(2)}, u32[]{:S(2)}) collective-permute-start(f32[40,512]{1,0:T(8,128)S(1)} %get-tuple-element.23), channel_id=1, source_target_pairs={{1,2},{3,4},{5,6},{7,0},{2,1},{4,3},{6,5},{0,7},{9,10},{11,12},{13... | collective-permute-start | bytes 245768 | tf_op jit(solution)/shard_map/ppermute | solution.py:802
  18.8 0.0 collective-permute-done.even_ref
  18.8 0.3 collective-permute-start.6
  19.1 0.0 collective-permute-done.5.rest_1_
  19.1 2.7 %collective-permute-start.7 = (f32[40,384]{1,0:T(8,128)S(1)}, f32[40,384]{1,0:T(8,128)S(1)}, u32[]{:S(2)}, u32[]{:S(2)}) collective-permute-start(f32[40,384]{1,0:T(8,128)S(1)} %get-tuple-element.29), channel_id=1, source_target_pairs={{0,6},{1,7},{2,4},{3,5},{4,2},{5,3},{6,0},{7,1},{8,14},{9,15},{10,... | collective-permute-start | bytes 184328 | tf_op jit(solution)/shard_map/ppermute | solution.py:805
  21.8 4.4 %cycle_planes_3.1.upper = f32[5,5,128,256]{3,2,1,0:T(8,128)S(1)} custom-call(f32[5,8,2,128,128]{4,3,2,1,0:T(8,128)S(1)} %get-tuple-element.16.q_ref, f32[40,384]{1,0:T(8,128)S(1)} %get-tuple-element.26.after.rest_0_), custom_call_target="tpu_custom_call" | custom-call | tf_op jit(solution)/shard_map/cycle_planes_3/pallas_call | solution.py:225
  26.2 0.0 collective-permute-done.6.rest_2_
  26.2 0.0 collective-permute-done.7.rest_3_
  26.2 0.0 collective-permute-done.2.odd_ref
  26.2 0.0 collective-permute-done.3.near_ref
  26.3 0.6 %collective-permute-done.4.far_ref = f32[5,152,256]{2,1,0:T(8,128)S(1)} collective-permute-done((f32[5,152,256]{2,1,0:T(8,128)S(1)}, f32[5,152,256]{2,1,0:T(8,128)S(1)}, u32[]{:S(2)}, u32[]{:S(2)}) %collective-permute-start.4) | collective-permute-done | bytes 778272 | tf_op jit(solution)/shard_map/ppermute | solution.py:797
  26.9 0.0 copy-done
  26.9 0.0 copy-done.1
  26.9 0.0 copy-done.2
  26.9 5.0 %late_terms.1 = (f32[5,8,128,256]{3,2,1,0:T(8,128)}, f32[5,8,24,192]{3,2,1,0:T(8,128)}) custom-call(f32[5,8,24,192]{3,2,1,0:T(8,128)S(1)} %copy-done, s32[4,768]{1,0:T(4,128)S(1)} %bitcast.4, f32[4,768]{1,0:T(4,128)S(1)} %bitcast.5, f32[40,512]{1,0:T(8,128)S(1)} %collective-permute-done.even_ref, f32[40,512]{1,0:T(8,128)S(1)} %collective-permute-done.2.odd_ref, ...), custom_call_target="tpu_custom_call" | custom-call | tf_op jit(solution)/shard_map/late_terms/pallas_call | solution.py:759
  (1 shorter events, 0.0 us)
Async XLA Ops:
  6.1 20.2 %collective-permute-start.3 = (f32[5,152,256]{2,1,0:T(8,128)S(1)}, f32[5,152,256]{2,1,0:T(8,128)S(1)}, u32[]{:S(2)}, u32[]{:S(2)}) collective-permute-start(f32[5,152,256]{2,1,0:T(8,128)S(1)} %get-tuple-element.24), channel_id=1, source_target_pairs={{0,8},{8,0},{16,24},{24,16},{1,9},{9,1},{17,25},{25,17},{2,10},{10... | collective-permute-start | bytes 2334728 | tf_op jit(solution)/shard_map/ppermute | solution.py:796
  6.6 20.3 %collective-permute-start.4 = (f32[5,152,256]{2,1,0:T(8,128)S(1)}, f32[5,152,256]{2,1,0:T(8,128)S(1)}, u32[]{:S(2)}, u32[]{:S(2)}) collective-permute-start(f32[5,152,256]{2,1,0:T(8,128)S(1)} %get-tuple-element.25), channel_id=1, source_target_pairs={{8,16},{24,0},{16,8},{0,24},{9,17},{25,1},{17,9},{1,25},{10,18},{2... | collective-permute-start | bytes 2334728 | tf_op jit(solution)/shard_map/ppermute | solution.py:797
  9.2 4.9 %collective-permute-start.1 = (f32[40,640]{1,0:T(8,128)S(1)}, f32[40,640]{1,0:T(8,128)S(1)}, u32[]{:S(2)}, u32[]{:S(2)}) collective-permute-start(f32[40,640]{1,0:T(8,128)S(1)} %get-tuple-element.19.sent), channel_id=1, source_target_pairs={{0,1},{1,0},{2,3},{3,2},{4,5},{5,4},{6,7},{7,6},{8,9},{9,8},{10,11... | collective-permute-start | bytes 307208 | tf_op jit(solution)/shard_map/ppermute | solution.py:795
  12.0 6.8 %collective-permute-start = (f32[40,512]{1,0:T(8,128)S(1)}, f32[40,512]{1,0:T(8,128)S(1)}, u32[]{:S(2)}, u32[]{:S(2)}) collective-permute-start(f32[40,512]{1,0:T(8,128)S(1)} %get-tuple-element.18), channel_id=1, source_target_pairs={{0,1},{1,0},{2,3},{3,2},{4,5},{5,4},{6,7},{7,6},{8,9},{9,8},{10,11... | collective-permute-start | bytes 245768 | tf_op jit(solution)/shard_map/ppermute | solution.py:800
  14.1 12.8 %copy-start = (f32[5,8,24,192]{3,2,1,0:T(8,128)S(1)}, f32[5,8,24,192]{3,2,1,0:T(8,128)}, u32[]{:S(2)}) copy-start(f32[5,8,24,192]{3,2,1,0:T(8,128)} %core_ref.1) | copy-start | bytes 2211844
  14.1 12.8 %copy-start.1 = (s32[768,4]{0,1:T(4,128)S(1)}, s32[768,4]{0,1:T(4,128)}, u32[]{:S(2)}) copy-start(s32[768,4]{0,1:T(4,128)} %param.8) | copy-start | bytes 36868
  14.1 12.8 %copy-start.2 = (f32[768,4]{0,1:T(4,128)S(1)}, f32[768,4]{0,1:T(4,128)}, u32[]{:S(2)}) copy-start(f32[768,4]{0,1:T(4,128)} %param.9) | copy-start | bytes 36868
  14.1 5.0 %collective-permute-start.5 = (f32[40,384]{1,0:T(8,128)S(1)}, f32[40,384]{1,0:T(8,128)S(1)}, u32[]{:S(2)}, u32[]{:S(2)}) collective-permute-start(f32[40,384]{1,0:T(8,128)S(1)} %get-tuple-element.27), channel_id=1, source_target_pairs={{0,2},{1,3},{2,0},{3,1},{4,6},{5,7},{6,4},{7,5},{8,10},{9,11},{10,... | collective-permute-start | bytes 184328 | tf_op jit(solution)/shard_map/ppermute | solution.py:805
  14.3 12.0 %collective-permute-start.2 = (f32[40,512]{1,0:T(8,128)S(1)}, f32[40,512]{1,0:T(8,128)S(1)}, u32[]{:S(2)}, u32[]{:S(2)}) collective-permute-start(f32[40,512]{1,0:T(8,128)S(1)} %get-tuple-element.23), channel_id=1, source_target_pairs={{1,2},{3,4},{5,6},{7,0},{2,1},{4,3},{6,5},{0,7},{9,10},{11,12},{13... | collective-permute-start | bytes 245768 | tf_op jit(solution)/shard_map/ppermute | solution.py:802
  18.8 7.4 %collective-permute-start.6 = (f32[40,384]{1,0:T(8,128)S(1)}, f32[40,384]{1,0:T(8,128)S(1)}, u32[]{:S(2)}, u32[]{:S(2)}) collective-permute-start(f32[40,384]{1,0:T(8,128)S(1)} %get-tuple-element.28), channel_id=1, source_target_pairs={{0,4},{1,5},{2,6},{3,7},{4,0},{5,1},{6,2},{7,3},{8,12},{9,13},{10,... | collective-permute-start | bytes 184328 | tf_op jit(solution)/shard_map/ppermute | solution.py:805
  19.1 7.1 %collective-permute-start.7 = (f32[40,384]{1,0:T(8,128)S(1)}, f32[40,384]{1,0:T(8,128)S(1)}, u32[]{:S(2)}, u32[]{:S(2)}) collective-permute-start(f32[40,384]{1,0:T(8,128)S(1)} %get-tuple-element.29), channel_id=1, source_target_pairs={{0,6},{1,7},{2,4},{3,5},{4,2},{5,3},{6,0},{7,1},{8,14},{9,15},{10,... | collective-permute-start | bytes 184328 | tf_op jit(solution)/shard_map/ppermute | solution.py:805
